TPU v7x, 32 devices: a whole 2x2x4 slice. The times are simulated.
32 devices in a mesh: dp: 8 (over y, x, core), tensor: 4 (over z).
Axes of the slice: x: 2, y: 2, z: 4, core: 2. Of those that a mesh axis runs over, the one named last changes fastest.
Arguments:
- tokens: bfloat16 [13056, 1024], P(('dp', 'tensor')), may hold values from -6 to 6
- lengths: int32 [25], replicated, may hold values from 32 to 1024, as said below
- gain_attn: float32 [1024], replicated, may hold values from 0.1 to 1.9
- w_qkv: bfloat16 [1024, 3, 1024], P(None, None, 'tensor'), may hold values from -0.1875 to 0.1875
- w_out: bfloat16 [1024, 1024], P('tensor'), may hold values from -1 to 1
- gain_ffn: float32 [1024], replicated, may hold values from 0.1 to 1.9
- w_in: bfloat16 [1024, 2, 2624], P(None, None, 'tensor'), may hold values from -0.1875 to 0.1875
- w_down: bfloat16 [2624, 1024], P('tensor'), may hold values from -0.15625 to 0.15625
- grad_output: bfloat16 [13056, 1024], P(('dp', 'tensor')), may hold values from -8 to 8
Outputs:
- output: bfloat16 [13056, 1024], P(('dp', 'tensor'))
- grad_tokens: bfloat16 [13056, 1024], P(('dp', 'tensor'))
- grad_gain_attn: float32 [1024], replicated
- grad_w_qkv: float32 [1024, 3, 1024], P('dp', None, 'tensor')
- grad_w_out: float32 [1024, 1024], P('tensor', 'dp')
- grad_gain_ffn: float32 [1024], replicated
- grad_w_in: float32 [1024, 2, 2624], P('dp', None, 'tensor')
- grad_w_down: float32 [2624, 1024], P('tensor', 'dp')
Inputs may be any that keep to these rules, and one draw needn't show every extreme that they name: The lengths sum to 13056. Document 0 starts at token 0; besides it, each aligned block of 544 tokens that starts at a multiple of 544 holds exactly one document start, at least 32 tokens after the run's first token and at most 512 after it.
All inputs are finite; a program needn't handle non-finite values.
Results may differ from a plain program's by a relative error of at most 0.024.
Values may be sent and summed in bfloat16 or wider, within the bound.
A program may use at most 128 MiB of HBM per device.

v0:
```python
import math

import jax
import jax.numpy as jnp
from jax import lax
from jax.sharding import PartitionSpec as P

D = 1024
HD = 64
HALF = 64
SPAN = 544


EPS = 1e-05
THETA = 10000.0


def extended(block, sides, width):
    for axis, dim in sides:
        count = lax.axis_size(axis)
        forward = [(i, i + 1) for i in range(count - 1)]
        backward = [(target, source) for source, target in forward]
        low = lax.ppermute(
            lax.slice_in_dim(block, block.shape[dim] - width, None, axis=dim), axis, forward
        )
        high = lax.ppermute(lax.slice_in_dim(block, 0, width, axis=dim), axis, backward)
        block = jnp.concatenate([low, block, high], axis=dim)
    return block


def layer_norm(values, gain_vec):
    center = values - jnp.mean(values, axis=-1, keepdims=True)
    spread = jnp.mean(center * center, axis=-1, keepdims=True)
    return center * lax.rsqrt(spread + EPS) * gain_vec


def layout(lengths, first, amount, total):
    places = first + jnp.arange(amount, dtype=jnp.int32)
    cuts = jnp.cumsum(lengths)[:-1]
    before = cuts[None, :] <= places[:, None]
    doc_ids = jnp.sum(before.astype(jnp.int32), axis=1)
    begins = jnp.max(jnp.where(before, cuts[None, :], 0), axis=1)
    positions = places - begins
    valid = (places >= 0) & (places < total)
    return (jnp.where(valid, doc_ids, -1), positions)


def rotary(positions):
    half_dim = HD // 2
    inverse = jnp.exp(jnp.arange(half_dim, dtype=jnp.float32) * (-2.0 * math.log(THETA) / HD))
    angles = positions.astype(jnp.float32)[:, None] * inverse[None, :]
    return (jnp.cos(angles)[:, None, :], jnp.sin(angles)[:, None, :])


def rotate(values, cosine, sine):
    half_dim = values.shape[-1] // 2
    first_half = values[..., :half_dim]
    second_half = values[..., half_dim:]
    return jnp.concatenate(
        [first_half * cosine - second_half * sine, second_half * cosine + first_half * sine],
        axis=-1,
    )


def gelu_product(hidden):
    return jax.nn.gelu(hidden[:, 0], approximate=False) * hidden[:, 1]


def window_scores(queries, keys_ext, seg_own, seg_ext, number, factor):
    offset = number * SPAN
    query_part = lax.dynamic_slice_in_dim(queries, offset, SPAN, 0)
    key_part = lax.dynamic_slice_in_dim(keys_ext, offset, SPAN + 2 * HALF, 0)
    seg_query = lax.dynamic_slice_in_dim(seg_own, offset, SPAN, 0)
    seg_key = lax.dynamic_slice_in_dim(seg_ext, offset, SPAN + 2 * HALF, 0)
    row_ids = jnp.arange(SPAN, dtype=jnp.int32)[:, None]
    col_ids = jnp.arange(SPAN + 2 * HALF, dtype=jnp.int32)[None, :]
    allowed = (jnp.abs(col_ids - HALF - row_ids) <= HALF) & (seg_query[:, None] == seg_key[None, :])
    scores = (
        jnp.einsum("qhd,khd->hqk", query_part, key_part, preferred_element_type=jnp.float32)
        * factor
    )
    return (query_part, key_part, allowed, scores)


def body(tokens, lengths, gain_attn, w_qkv, w_out, gain_ffn, w_in, w_down, grad_output):
    own_rows = tokens.shape[0]
    tok_block = own_rows * lax.axis_size("tensor")
    total = tok_block * lax.axis_size("dp")
    local_heads = w_qkv.shape[2] // HD
    width_heads = local_heads * HD
    blocks_num = tok_block // SPAN
    factor = 1.0 / math.sqrt(HD)
    block_start = lax.axis_index("dp") * tok_block
    x_own = tokens.astype(jnp.float32)
    normed_own, norm_pull_one = jax.vjp(layer_norm, x_own, gain_attn)
    normed_full = lax.all_gather(normed_own.astype(jnp.bfloat16), "tensor", axis=0, tiled=True)
    projected = jnp.dot(
        normed_full, w_qkv.reshape(D, 3 * width_heads), preferred_element_type=jnp.float32
    )
    projected = projected.reshape(tok_block, 3, local_heads, HD)
    seg_ext, pos_ext = layout(lengths, block_start - HALF, tok_block + 2 * HALF, total)
    seg_own = seg_ext[HALF : HALF + tok_block]
    cosine, sine = rotary(pos_ext[HALF : HALF + tok_block])

    def rope_all(raw_values):
        return (
            rotate(raw_values[:, 0], cosine, sine),
            rotate(raw_values[:, 1], cosine, sine),
            raw_values[:, 2],
        )

    (query_rot, key_rot, value_raw), rope_pull = jax.vjp(rope_all, projected)
    query_low = query_rot.astype(jnp.bfloat16)
    pair_low = jnp.concatenate(
        [
            key_rot.astype(jnp.bfloat16).reshape(tok_block, width_heads),
            value_raw.astype(jnp.bfloat16).reshape(tok_block, width_heads),
        ],
        axis=1,
    )
    pair_ext = extended(pair_low, (("dp", 0),), HALF)
    key_ext = pair_ext[:, :width_heads].reshape(-1, local_heads, HD)
    value_ext = pair_ext[:, width_heads:].reshape(-1, local_heads, HD)

    def attend_forward(number):
        query_part, key_part, allowed, scores = window_scores(
            query_low, key_ext, seg_own, seg_ext, number, factor
        )
        value_part = lax.dynamic_slice_in_dim(value_ext, number * SPAN, SPAN + 2 * HALF, 0)
        masked = jnp.where(allowed[None], scores, -1e30)
        row_max = jnp.max(masked, axis=-1, keepdims=True)
        raised = jnp.exp(masked - row_max)
        row_sum = jnp.sum(raised, axis=-1, keepdims=True)
        probs = (raised / row_sum).astype(jnp.bfloat16)
        mixed_part = jnp.einsum(
            "hqk,khd->qhd", probs, value_part, preferred_element_type=jnp.float32
        )
        return (mixed_part.astype(jnp.bfloat16), (row_max + jnp.log(row_sum))[..., 0])

    mixed_all, log_totals = lax.map(attend_forward, jnp.arange(blocks_num, dtype=jnp.int32))
    mixed_low = mixed_all.reshape(tok_block, width_heads)
    residual = x_own + lax.psum_scatter(
        jnp.dot(mixed_low, w_out, preferred_element_type=jnp.float32).astype(jnp.bfloat16),
        "tensor",
        scatter_dimension=0,
        tiled=True,
    ).astype(jnp.float32)
    normed_ffn, norm_pull_two = jax.vjp(layer_norm, residual, gain_ffn)
    normed_ffn_low = normed_ffn.astype(jnp.bfloat16)
    weight_in, weight_down = (w_in, w_down)
    rows_in = lax.all_gather(normed_ffn_low, "tensor", axis=0, tiled=True)
    hidden_units = weight_in.shape[2]
    hidden = jnp.dot(
        rows_in, weight_in.reshape(D, 2 * hidden_units), preferred_element_type=jnp.float32
    )
    activated, gelu_pull = jax.vjp(gelu_product, hidden.reshape(-1, 2, hidden_units))
    act_low = activated.astype(jnp.bfloat16)
    ffn_own = lax.psum_scatter(
        jnp.dot(act_low, weight_down, preferred_element_type=jnp.float32).astype(jnp.bfloat16),
        "tensor",
        scatter_dimension=0,
        tiled=True,
    ).astype(jnp.float32)
    output = (residual + ffn_own).astype(jnp.bfloat16)
    grad_out32 = grad_output.astype(jnp.float32)
    grad_low = grad_out32.astype(jnp.bfloat16)
    grad_rows = lax.all_gather(grad_low, "tensor", axis=0, tiled=True)
    grad_down = jnp.einsum("tf,td->fd", act_low, grad_rows, preferred_element_type=jnp.float32)
    grad_act = jnp.einsum("td,fd->tf", grad_rows, weight_down, preferred_element_type=jnp.float32)
    (grad_hidden,) = gelu_pull(grad_act)
    grad_hidden_low = grad_hidden.astype(jnp.bfloat16).reshape(-1, 2 * hidden_units)
    grad_in = jnp.einsum(
        "td,tf->df", rows_in, grad_hidden_low, preferred_element_type=jnp.float32
    ).reshape(D, 2, hidden_units)
    part_rows = grad_hidden_low
    grad_normed_ffn = lax.psum_scatter(
        jnp.einsum(
            "tf,df->td",
            part_rows,
            w_in.reshape(D, 2 * hidden_units),
            preferred_element_type=jnp.float32,
        ).astype(jnp.bfloat16),
        "tensor",
        scatter_dimension=0,
        tiled=True,
    ).astype(jnp.float32)
    grad_resid_part, grad_gain_two = norm_pull_two(grad_normed_ffn)
    grad_residual = grad_out32 + grad_resid_part
    grad_res_full = lax.all_gather(grad_residual.astype(jnp.bfloat16), "tensor", axis=0, tiled=True)
    grad_wout = jnp.einsum(
        "tc,td->cd", mixed_low, grad_res_full, preferred_element_type=jnp.float32
    )
    grad_mixed = jnp.einsum("td,cd->tc", grad_res_full, w_out, preferred_element_type=jnp.float32)
    grad_mixed = grad_mixed.astype(jnp.bfloat16).reshape(tok_block, local_heads, HD)

    def attend_backward(running, number):
        grad_key_ext, grad_value_ext = running
        query_part, key_part, allowed, scores = window_scores(
            query_low, key_ext, seg_own, seg_ext, number, factor
        )
        offset = number * SPAN
        value_part = lax.dynamic_slice_in_dim(value_ext, offset, SPAN + 2 * HALF, 0)
        grad_part = lax.dynamic_slice_in_dim(grad_mixed, offset, SPAN, 0)
        log_part = log_totals[number]
        probs = jnp.where(allowed[None], jnp.exp(scores - log_part[..., None]), 0.0)
        grad_probs = jnp.einsum(
            "qhd,khd->hqk", grad_part, value_part, preferred_element_type=jnp.float32
        )
        centre_term = jnp.sum(probs * grad_probs, axis=-1, keepdims=True)
        grad_scores = (probs * (grad_probs - centre_term)).astype(jnp.bfloat16)
        grad_query = (
            jnp.einsum("hqk,khd->qhd", grad_scores, key_part, preferred_element_type=jnp.float32)
            * factor
        )
        grad_key = (
            jnp.einsum("hqk,qhd->khd", grad_scores, query_part, preferred_element_type=jnp.float32)
            * factor
        )
        grad_value = jnp.einsum(
            "hqk,qhd->khd",
            probs.astype(jnp.bfloat16),
            grad_part,
            preferred_element_type=jnp.float32,
        )
        old_key = lax.dynamic_slice_in_dim(grad_key_ext, offset, SPAN + 2 * HALF, 0)
        old_value = lax.dynamic_slice_in_dim(grad_value_ext, offset, SPAN + 2 * HALF, 0)
        grad_key_ext = lax.dynamic_update_slice_in_dim(grad_key_ext, old_key + grad_key, offset, 0)
        grad_value_ext = lax.dynamic_update_slice_in_dim(
            grad_value_ext, old_value + grad_value, offset, 0
        )
        return ((grad_key_ext, grad_value_ext), grad_query)

    zeros_ext = jnp.zeros((tok_block + 2 * HALF, local_heads, HD), jnp.float32)
    (grad_key_ext, grad_value_ext), grad_queries = lax.scan(
        attend_backward, (zeros_ext, zeros_ext), jnp.arange(blocks_num, dtype=jnp.int32)
    )
    grad_pair_ext = jnp.concatenate(
        [grad_key_ext.reshape(-1, width_heads), grad_value_ext.reshape(-1, width_heads)], axis=1
    )
    rim_grads = jnp.concatenate([grad_pair_ext[:HALF], grad_pair_ext[-HALF:]], axis=0)
    rim_back = extended(rim_grads.astype(jnp.bfloat16), (("dp", 0),), HALF).astype(rim_grads.dtype)
    from_before = rim_back[:HALF]
    from_after = rim_back[-HALF:]
    grad_pair = grad_pair_ext[HALF : HALF + tok_block]
    grad_pair = (
        grad_pair
        + jnp.pad(from_before, ((0, tok_block - HALF), (0, 0)))
        + jnp.pad(from_after, ((tok_block - HALF, 0), (0, 0)))
    )
    grad_keys = grad_pair[:, :width_heads].reshape(tok_block, local_heads, HD)
    grad_values = grad_pair[:, width_heads:].reshape(tok_block, local_heads, HD)
    grad_queries = grad_queries.reshape(tok_block, local_heads, HD)
    (grad_projected,) = rope_pull((grad_queries, grad_keys, grad_values))
    grad_qkv_low = grad_projected.astype(jnp.bfloat16).reshape(tok_block, 3 * width_heads)
    grad_qkv = jnp.einsum(
        "td,tc->dc", normed_full, grad_qkv_low, preferred_element_type=jnp.float32
    ).reshape(D, 3, width_heads)
    part_rows = grad_qkv_low
    grad_normed = lax.psum_scatter(
        jnp.einsum(
            "tc,dc->td",
            part_rows,
            w_qkv.reshape(D, 3 * width_heads),
            preferred_element_type=jnp.float32,
        ).astype(jnp.bfloat16),
        "tensor",
        scatter_dimension=0,
        tiled=True,
    ).astype(jnp.float32)
    grad_x_part, grad_gain_one = norm_pull_one(grad_normed)
    grad_tokens = (grad_residual + grad_x_part).astype(jnp.bfloat16)
    gain_one_sum, gain_two_sum = lax.psum((grad_gain_one, grad_gain_two), ("dp", "tensor"))
    qkv_sum, wout_sum, in_sum, down_sum = (
        lax.psum_scatter(grad_qkv, "dp", scatter_dimension=0, tiled=True),
        lax.psum_scatter(grad_wout, "dp", scatter_dimension=1, tiled=True),
        lax.psum_scatter(grad_in, "dp", scatter_dimension=0, tiled=True),
        lax.psum_scatter(grad_down, "dp", scatter_dimension=1, tiled=True),
    )
    return (output, grad_tokens, gain_one_sum, qkv_sum, wout_sum, gain_two_sum, in_sum, down_sum)


def solution(mesh):
    in_specs = (
        P(("dp", "tensor"), None),
        P(),
        P(),
        P(None, None, "tensor"),
        P("tensor", None),
        P(),
        P(None, None, "tensor"),
        P("tensor", None),
        P(("dp", "tensor"), None),
    )
    out_specs = (
        P(("dp", "tensor"), None),
        P(("dp", "tensor"), None),
        P(),
        P("dp", None, "tensor"),
        P("tensor", "dp"),
        P(),
        P("dp", None, "tensor"),
        P("tensor", "dp"),
    )
    return jax.shard_map(body, mesh=mesh, in_specs=in_specs, out_specs=out_specs, check_vma=False)
```

profile of v0, /device:TPU:0, one launch (start us, length us, event | category | flops | bytes accessed | tf_op | source)
XLA Modules:
  0.0 1033.7 jit_solution(1605174445096481865)
XLA Ops:
  16.8 65.5 %all-gather.5.cloned.1.call-done = bf16[1632,1024]{1,0:T(8,128)(2,1)} async-done(((bf16[408,1024]{1,0:T(8,128)(2,1)}), bf16[1632,1024]{1,0:T(8,128)(2,1)}) %all-gather.5.cloned.1.call-update) | async-done | bytes 3342352 | tf_op jit(solution)/shard_map/all_gather | solution.py:96
  82.3 5.5 fusion.71
  96.0 4.4 concatenate.25
  103.3 35.3 %while.30 = (s32[]{:T(128)}, bf16[3,544,4,64]{1,3,2,0:T(8,128)(2,1)}, f32[3,4,544]{2,1,0:T(4,128)}, s32[3]{0:T(128)S(1)}, bf16[1760,4,64]{0,2,1:T(8,128)(2,1)}, ...) while((s32[]{:T(128)}, ...), condition=%wide.region_8.9_spmd, body=%wide.region_5.8_spmd.sunk | while | flops 393854496 | bytes 20543724 | solution.py:140
  111.0 4.1 fusion.156
  122.7 4.1 fusion.156
  134.5 4.1 fusion.156
  145.4 4.0 convolution_convert_fusion.2
  150.2 64.5 %reduce-scatter.9.cloned.1.call-done = bf16[408,1024]{1,0:T(8,128)(2,1)} async-done(((bf16[1632,1024]{1,0:T(8,128)(2,1)}), bf16[408,1024]{1,0:T(8,128)(2,1)}) %reduce-scatter.9.cloned.1.call-update) | async-done | bytes 835600 | tf_op jit(solution)/shard_map/reduce_scatter | solution.py:142
  219.5 63.7 %all-gather.9.cloned.1.call-done = bf16[1632,1024]{1,0:T(8,128)(2,1)} async-done(((bf16[408,1024]{1,0:T(8,128)(2,1)}), bf16[1632,1024]{1,0:T(8,128)(2,1)}) %all-gather.9.cloned.1.call-update) | async-done | bytes 3342352 | tf_op jit(solution)/shard_map/all_gather | solution.py:167
  283.2 7.0 fusion.112
  290.2 60.5 %all-gather.7.cloned.1.call-done = bf16[1632,1024]{1,0:T(8,128)(2,1)} async-done(((bf16[408,1024]{1,0:T(8,128)(2,1)}), bf16[1632,1024]{1,0:T(8,128)(2,1)}) %all-gather.7.cloned.1.call-update) | async-done | bytes 3342352 | tf_op jit(solution)/shard_map/all_gather | solution.py:151
  350.7 7.2 fusion.76
  357.9 9.3 multiply_bitcast_fusion
  372.6 7.0 bitcast_convert_fusion
  381.3 5.9 convolution_convert_fusion.1
  387.2 54.5 %reduce-scatter.13.cloned.1.call-done = bf16[408,1024]{1,0:T(8,128)(2,1)} async-done(((bf16[1632,1024]{1,0:T(8,128)(2,1)}), bf16[408,1024]{1,0:T(8,128)(2,1)}) %reduce-scatter.13.cloned.1.call-update) | async-done | bytes 835600 | tf_op jit(solution)/shard_map/reduce_scatter | solution.py:176
  444.3 63.1 %reduce-scatter.11.cloned.1.call-done = bf16[408,1024]{1,0:T(8,128)(2,1)} async-done(((bf16[1632,1024]{1,0:T(8,128)(2,1)}), bf16[408,1024]{1,0:T(8,128)(2,1)}) %reduce-scatter.11.cloned.1.call-update) | async-done | bytes 835600 | tf_op jit(solution)/shard_map/reduce_scatter | solution.py:158
  513.7 66.8 %all-gather.11.cloned.1.call-done = bf16[1632,1024]{1,0:T(8,128)(2,1)} async-done(((bf16[408,1024]{1,0:T(8,128)(2,1)}), bf16[1632,1024]{1,0:T(8,128)(2,1)}) %all-gather.11.cloned.1.call-update) | async-done | bytes 3342352 | tf_op jit(solution)/shard_map/all_gather | solution.py:189
  580.6 3.9 convolution_convert_fusion.3
  589.5 151.4 %while.31 = (s32[]{:T(128)}, f32[1760,4,64]{0,2,1:T(8,128)}, f32[1760,4,64]{0,2,1:T(8,128)}, f32[3,544,4,64]{1,0,3,2:T(4,128)}, s32[3]{0:T(128)S(1)}, /*index=5*...) while((s32[]{:T(128)}, f32[1760,4,64]{0,2,1:T(8,128)}, ...), condition=%wide.region_18.19_spmd, body=%wide.region_16.18_spmd.sunk | while | flops 960269824 | bytes 90647960 | solution.py:234
  590.7 5.0 fusion.165
  599.1 6.2 multiply_reduce_fusion.3
  610.8 13.5 %dynamic_update_slice.44 = f32[3,544,4,64]{1,0,3,2:T(4,128)} dynamic-update-slice(f32[3,544,4,64]{1,0,3,2:T(4,128)} %get-tuple-element.578, f32[1,544,4,64]{1,0,3,2:T(1,128)S(1)} %copy.58, s32[]{:T(128)} %get-tuple-element.575, s32[]{:T(128)} %constant.186.clone.1..sunk.1, s32[]{:T(128)} %constant.186.clone.1..sunk.1, s32[]{:T(128)} %constant.186.clone.1..sunk.1) | dynamic-update-slice | bytes 1114116 | tf_op jit(solution)/shard_map/while/body/jit(dynamic_update_index_in_dim)/dynamic_update_slice | solution.py:234
  627.5 3.7 dynamic_update_slice.42
  631.2 4.9 fusion.168
  636.1 3.7 dynamic_update_slice.43
  641.0 5.0 fusion.165
  649.4 6.2 multiply_reduce_fusion.3
  661.1 13.5 %dynamic_update_slice.44 = f32[3,544,4,64]{1,0,3,2:T(4,128)} dynamic-update-slice(f32[3,544,4,64]{1,0,3,2:T(4,128)} %get-tuple-element.578, f32[1,544,4,64]{1,0,3,2:T(1,128)S(1)} %copy.58, s32[]{:T(128)} %get-tuple-element.575, s32[]{:T(128)} %constant.186.clone.1..sunk.1, s32[]{:T(128)} %constant.186.clone.1..sunk.1, s32[]{:T(128)} %constant.186.clone.1..sunk.1) | dynamic-update-slice | bytes 1114116 | tf_op jit(solution)/shard_map/while/body/jit(dynamic_update_index_in_dim)/dynamic_update_slice | solution.py:234
  677.7 4.1 dynamic_update_slice.42
  681.9 4.9 fusion.168
  686.8 4.2 dynamic_update_slice.43
  692.2 5.0 fusion.165
  700.5 6.1 multiply_reduce_fusion.3
  712.2 13.5 %dynamic_update_slice.44 = f32[3,544,4,64]{1,0,3,2:T(4,128)} dynamic-update-slice(f32[3,544,4,64]{1,0,3,2:T(4,128)} %get-tuple-element.578, f32[1,544,4,64]{1,0,3,2:T(1,128)S(1)} %copy.58, s32[]{:T(128)} %get-tuple-element.575, s32[]{:T(128)} %constant.186.clone.1..sunk.1, s32[]{:T(128)} %constant.186.clone.1..sunk.1, s32[]{:T(128)} %constant.186.clone.1..sunk.1) | dynamic-update-slice | bytes 1114116 | tf_op jit(solution)/shard_map/while/body/jit(dynamic_update_index_in_dim)/dynamic_update_slice | solution.py:234
  732.4 4.8 fusion.168
  746.5 4.2 reshape.345
  757.7 4.3 convolution_convert_fusion
  763.6 6.0 fusion.114
  769.7 10.1 fusion.46
  780.9 4.1 fusion.113
  785.4 7.6 fusion.73
  793.0 33.7 %reduce-scatter.15.cloned.1.call-done = bf16[408,1024]{1,0:T(8,128)(2,1)} async-done(((bf16[1632,1024]{1,0:T(8,128)(2,1)}), bf16[408,1024]{1,0:T(8,128)(2,1)}) %reduce-scatter.15.cloned.1.call-update) | async-done | bytes 835600 | tf_op jit(solution)/shard_map/reduce_scatter | solution.py:259
  830.6 40.5 %all-reduce.11 = (f32[1024]{0:T(1024)}, f32[1024]{0:T(1024)}) all-reduce(f32[1024]{0:T(1024)S(1)} %get-tuple-element.292, f32[1024]{0:T(1024)S(1)} %copy-done.34), channel_id=1, replica_groups=mesh['dp'=8,'tensor'=4] {'dp','tensor'}, use_global_device_ids=true, to_apply=%region_23.24 | all-reduce | flops 2048 | bytes 16384 | tf_op jit(solution)/shard_map/psum | solution.py:272
  875.6 61.2 %reduce-scatter.21.cloned.1.call-done = f32[128,2,656]{0,2,1:T(8,128)} async-done(((f32[1024,2,656]{0,2,1:T(8,128)}), f32[128,2,656]{0,2,1:T(8,128)}) %reduce-scatter.21.cloned.1.call-update) | async-done | bytes 671760 | tf_op jit(solution)/shard_map/reduce_scatter | solution.py:276
  936.8 39.8 %reduce-scatter.19.cloned.1.call-done = f32[256,128]{1,0:T(8,128)} async-done(((f32[256,1024]{1,0:T(8,128)}), f32[256,128]{1,0:T(8,128)}) %reduce-scatter.19.cloned.1.call-update) | async-done | bytes 131088 | tf_op jit(solution)/shard_map/reduce_scatter | solution.py:275
  976.5 50.1 %reduce-scatter.17.cloned.1.call-done = f32[128,3,256]{2,0,1:T(8,128)} async-done(((f32[1024,3,256]{2,0,1:T(8,128)}), f32[128,3,256]{2,0,1:T(8,128)}) %reduce-scatter.17.cloned.1.call-update) | async-done | bytes 393232 | tf_op jit(solution)/shard_map/reduce_scatter | solution.py:274
  (239 shorter events, 138.0 us)
Async XLA Ops:
  7.2 343.6 %copy-start = (bf16[1024,2,656]{0,2,1:T(8,128)(2,1)S(1)}, bf16[1024,2,656]{0,2,1:T(8,128)(2,1)}, u32[]{:S(2)}) copy-start(bf16[1024,2,656]{0,2,1:T(8,128)(2,1)} %param.19) | copy-start | bytes 8060932
  7.2 75.1 %all-gather.5.cloned.1.call-start = ((), (), s32[]{:S(2)}) async-start(), calls=%async_computation.8 | async-start | bytes 4177920 | tf_op jit(solution)/shard_map/all_gather | solution.py:96
  8.7 6.6 copy-start.35
  8.7 7.1 copy-start.26
  10.3 5.1 copy-start.32
  10.3 5.1 copy-start.30
  12.7 202.0 %reduce-scatter.9.cloned.1.call-start = ((), (), s32[]{:S(2)}) async-start(), calls=%async_computation.9 | async-start | bytes 4177920 | tf_op jit(solution)/shard_map/reduce_scatter | solution.py:142
  16.8 71.3 %copy-start.18 = (f32[1632,32]{0,1:T(8,128)}, f32[1632,32]{0,1:T(8,128)S(1)}, u32[]{:S(2)}) copy-start(f32[1632,32]{0,1:T(8,128)S(1)} %get-tuple-element.375) | copy-start | bytes 626692
  16.8 71.3 %copy-start.20 = (f32[1632,32]{0,1:T(8,128)}, f32[1632,32]{0,1:T(8,128)S(1)}, u32[]{:S(2)}) copy-start(f32[1632,32]{0,1:T(8,128)S(1)} %get-tuple-element.376) | copy-start | bytes 626692
  89.8 4.5 collective-permute-start
  91.5 4.5 collective-permute-start.1
  138.6 6.8 copy-start.23
  149.4 65.3 %copy-start.3 = (bf16[408,1024]{1,0:T(8,128)(2,1)S(1)}, bf16[408,1024]{1,0:T(8,128)(2,1)}, u32[]{:S(2)}) copy-start(bf16[408,1024]{1,0:T(8,128)(2,1)} %param.13) | copy-start | bytes 2506756
  149.4 68.4 %copy-start.29 = (f32[1024]{0:T(1024)S(1)}, f32[1024]{0:T(1024)}, u32[]{:S(2)}) copy-start(f32[1024]{0:T(1024)} %param.18) | copy-start | bytes 12292
  149.4 133.9 %all-gather.9.cloned.1.call-start = ((), (), s32[]{:S(2)}) async-start(), calls=%async_computation.12 | async-start | bytes 4177920 | tf_op jit(solution)/shard_map/all_gather | solution.py:167
  150.1 200.6 %all-gather.7.cloned.1.call-start = ((), (), s32[]{:S(2)}) async-start(), calls=%async_computation.10 | async-start | bytes 4177920 | tf_op jit(solution)/shard_map/all_gather | solution.py:151
  214.7 3.1 copy-start.6
  219.1 222.7 %reduce-scatter.13.cloned.1.call-start = ((), (), s32[]{:S(2)}) async-start(), calls=%async_computation.13 | async-start | bytes 4177920 | tf_op jit(solution)/shard_map/reduce_scatter | solution.py:176
  350.7 7.2 copy-start.8
  367.3 3.3 copy-start.13
  370.6 2.1 copy-start.14
  379.7 127.8 %reduce-scatter.11.cloned.1.call-start = ((), (), s32[]{:S(2)}) async-start(), calls=%async_computation.11 | async-start | bytes 4177920 | tf_op jit(solution)/shard_map/reduce_scatter | solution.py:158
  387.1 54.6 %copy-start.7 = (bf16[408,1024]{1,0:T(8,128)(2,1)S(1)}, bf16[408,1024]{1,0:T(8,128)(2,1)}, u32[]{:S(2)}) copy-start(bf16[408,1024]{1,0:T(8,128)(2,1)} %reduce-scatter.9.cloned.1.call-done) | copy-start | bytes 2506756
  387.2 193.4 %all-gather.11.cloned.1.call-start = ((), (), s32[]{:S(2)}) async-start(), calls=%async_computation.14 | async-start | bytes 4177920 | tf_op jit(solution)/shard_map/all_gather | solution.py:189
  510.5 70.0 %copy-start.10 = (f32[408,1024]{1,0:T(8,128)}, f32[408,1024]{1,0:T(8,128)S(1)}, u32[]{:S(2)}) copy-start(f32[408,1024]{1,0:T(8,128)S(1)} %get-tuple-element.341) | copy-start | bytes 5013508
  510.5 70.0 %copy-start.24 = (bf16[256,1024]{1,0:T(8,128)(2,1)S(1)}, bf16[256,1024]{1,0:T(8,128)(2,1)}, u32[]{:S(2)}) copy-start(bf16[256,1024]{1,0:T(8,128)(2,1)} %param.17) | copy-start | bytes 1572868
  513.5 313.2 %reduce-scatter.15.cloned.1.call-start = ((), (), s32[]{:S(2)}) async-start(), calls=%async_computation.15 | async-start | bytes 4177920 | tf_op jit(solution)/shard_map/reduce_scatter | solution.py:259
  584.5 5.0 copy-start.4
  599.1 6.2 slice-start
  599.1 6.2 slice-start.1
  649.4 6.2 slice-start
  649.4 6.2 slice-start.1
  700.5 6.2 slice-start
  700.5 6.2 slice-start.1
  743.2 9.5 copy-start.5
  743.2 7.6 collective-permute-start.2
  745.0 6.4 collective-permute-start.3
  750.7 2.0 copy-start.9
  762.0 113.5 %reduce-scatter.23.cloned.1.call-start = ((), (), s32[]{:S(2)}) async-start(), calls=%async_computation.19 | async-start | bytes 3022848 | tf_op jit(solution)/shard_map/reduce_scatter | solution.py:277
  769.7 167.1 %reduce-scatter.21.cloned.1.call-start = ((), (), s32[]{:S(2)}) async-start(), calls=%async_computation.18 | async-start | bytes 6045696 | tf_op jit(solution)/shard_map/reduce_scatter | solution.py:276
  779.8 196.7 %reduce-scatter.19.cloned.1.call-start = ((), (), s32[]{:S(2)}) async-start(), calls=%async_computation.17 | async-start | bytes 1179648 | tf_op jit(solution)/shard_map/reduce_scatter | solution.py:275
  785.1 241.5 %reduce-scatter.17.cloned.1.call-start = ((), (), s32[]{:S(2)}) async-start(), calls=%async_computation.16 | async-start | bytes 3538944 | tf_op jit(solution)/shard_map/reduce_scatter | solution.py:274
  785.4 41.3 %copy-start.27 = (f32[408]{0:T(512)S(1)}, f32[408]{0:T(512)}, u32[]{:S(2)}) copy-start(f32[408]{0:T(512)} %copy-done.26) | copy-start | bytes 4900
  785.4 41.3 %copy-start.28 = (f32[1024]{0:T(1024)S(1)}, f32[1024]{0:T(1024)}, u32[]{:S(2)}) copy-start(f32[1024]{0:T(1024)} %param.15) | copy-start | bytes 12292
  793.0 35.3 %copy-start.33 = (f32[408]{0:T(512)S(1)}, f32[408]{0:T(512)}, u32[]{:S(2)}) copy-start(f32[408]{0:T(512)} %copy-done.32) | copy-start | bytes 4900
  793.0 35.3 %copy-start.31 = (f32[408]{0:T(512)S(1)}, f32[408]{0:T(512)}, u32[]{:S(2)}) copy-start(f32[408]{0:T(512)} %copy-done.30) | copy-start | bytes 4900
  793.0 37.6 %copy-start.34 = (f32[1024]{0:T(1024)S(1)}, f32[1024]{0:T(1024)}, u32[]{:S(2)}) copy-start(f32[1024]{0:T(1024)} %get-tuple-element.290) | copy-start | bytes 12292
  828.3 198.3 %copy-start.1 = (bf16[1024,2,656]{0,2,1:T(8,128)(2,1)S(1)}, bf16[1024,2,656]{0,2,1:T(8,128)(2,1)}, u32[]{:S(2)}) copy-start(bf16[1024,2,656]{0,2,1:T(8,128)(2,1)} %param.19) | copy-start | bytes 8060932
  (12 other events, 18.0 us)
Sparse Core Ops, SparseCore 0:
  12.8 69.4 all-gather.4
  149.5 65.1 reduce-scatter.8
  216.3 66.8 all-gather.8
  285.3 65.3 all-gather.6
  379.8 61.9 reduce-scatter.12
  443.9 63.4 reduce-scatter.10
  513.6 66.8 all-gather.10
  762.2 64.4 reduce-scatter.14
  830.7 44.8 reduce-scatter.22
  879.4 57.3 reduce-scatter.20
  940.5 35.9 reduce-scatter.18
  980.4 46.2 reduce-scatter.16
where the time goes:
time: 1040 us; the launch traced here: 1030 us
  waiting for transfers between devices  627 us (60%)
  matrix products  155 us (15%)
  local copies, waits for them, and re-layouts  114 us (11%)
  other arithmetic  64.9 us (6%)
  blocking collectives  40.5 us (4%)
  between operations  14.9 us (1%)
    all_gather x1, waiting for transfers between devices, body(): lax.all_gather(grad_residual.astype(jnp.bfloat16), 'tensor', axis=0, tile...  66.8 us
    all_gather x1, waiting for transfers between devices, body(): lax.all_gather(normed_own.astype(jnp.bfloat16), 'tensor', axis=0, tiled=T...  65.5 us
    reduce_scatter x1, waiting for transfers between devices, body(): lax.psum_scatter(jnp.dot(mixed_low, w_out, preferred_element_type=jnp.flo...  64.5 us
    all_gather x1, waiting for transfers between devices, body(): grad_rows = lax.all_gather(grad_low, 'tensor', axis=0, tiled=True)  63.7 us
    reduce_scatter x1, waiting for transfers between devices, body(): lax.psum_scatter(jnp.dot(act_low, weight_down, preferred_element_type=jnp...  63.1 us
    reduce_scatter x1, waiting for transfers between devices, body(): lax.psum_scatter(grad_in, 'dp', scatter_dimension=0, tiled=True)  61.2 us
    all_gather x1, waiting for transfers between devices, body(): rows_in = lax.all_gather(normed_ffn_low, 'tensor', axis=0, tiled=True)  60.5 us
    reduce_scatter x1, waiting for transfers between devices, body(): lax.psum_scatter(jnp.einsum('tf,df->td', part_rows, w_in.reshape(D, 2 * h...  54.5 us
  transfers between devices with their start and end apart: 16, of which 13 were waited for; matrix products, arithmetic and copies ran while one was open for 6% of the time, Pallas kernels for 0%

commit v1 on v0

v1 whole, which is shorter than its diff:
```python
import math

import jax
import jax.numpy as jnp
from jax import lax
from jax.experimental import pallas as pl
from jax.experimental.pallas import tpu as pltpu
from jax.sharding import PartitionSpec as P

D = 1024
HD = 64
HALF = 64
LANES = 128
EPS = 1e-05
THETA = 10000.0
ROWS = ("dp", "tensor")
PIECES = ("tensor", "dp")
BF = jnp.bfloat16
F32 = jnp.float32


def layer_norm(values, gain_vec):
    center = values - jnp.mean(values, axis=-1, keepdims=True)
    spread = jnp.mean(center * center, axis=-1, keepdims=True)
    return center * lax.rsqrt(spread + EPS) * gain_vec


def layout(lengths, first, amount, total):
    places = first + jnp.arange(amount, dtype=jnp.int32)
    cuts = jnp.cumsum(lengths)[:-1]
    before = cuts[None, :] <= places[:, None]
    doc_ids = jnp.sum(before.astype(jnp.int32), axis=1)
    begins = jnp.max(jnp.where(before, cuts[None, :], 0), axis=1)
    positions = places - begins
    valid = (places >= 0) & (places < total)
    return (jnp.where(valid, doc_ids, -1), positions)


def rotary(positions):
    half_dim = HD // 2
    inverse = jnp.exp(jnp.arange(half_dim, dtype=F32) * (-2.0 * math.log(THETA) / HD))
    angles = positions.astype(F32)[:, None] * inverse[None, :]
    cosine, sine = jnp.cos(angles), jnp.sin(angles)
    return (
        jnp.concatenate([cosine] * 4, axis=1),
        jnp.concatenate([-sine, sine, -sine, sine], axis=1),
    )


def dot(a, b, dims):
    return lax.dot_general(a, b, (dims, ((), ())), preferred_element_type=F32)


NT = ((1,), (1,))
NN = ((1,), (0,))
TN = ((0,), (0,))


def swap(u):
    lane = lax.broadcasted_iota(jnp.int32, u.shape, 1)
    return jnp.where((lane & 32) == 0, pltpu.roll(u, 96, 1), pltpu.roll(u, 32, 1))


def cut_blocks(rows):
    count = max(rows // LANES, 1)
    return [
        (i * LANES, LANES if i < count - 1 else rows - (count - 1) * LANES) for i in range(count)
    ]


def head_masks(rows):
    lane = lax.broadcasted_iota(jnp.int32, (rows, LANES), 1)
    return ((lane < HD).astype(F32), (lane >= HD).astype(F32))


def load_qkv(rows, q_ref, k_ref, v_ref, c_ref, s_ref):
    cosine, sine = c_ref[...], s_ref[...]
    q = q_ref[0, HALF : HALF + rows, :]
    q = q * cosine[HALF : HALF + rows] + swap(q) * sine[HALF : HALF + rows]
    q = q.astype(BF).astype(F32) * (1.0 / math.sqrt(HD))
    k = k_ref[0]
    k = (k * cosine + swap(k) * sine).astype(BF)
    return q, k, v_ref[0].astype(BF), cosine, sine


def soft(qh, kw, bias):
    scores = dot(qh, kw, NT) + bias
    raised = jnp.exp(scores - jnp.max(scores, axis=1, keepdims=True))
    return raised * (1.0 / jnp.sum(raised, axis=1, keepdims=True))


def fwd_kernel(rows, q_ref, k_ref, v_ref, c_ref, s_ref, b_ref, o_ref):
    q, k, v, _, _ = load_qkv(rows, q_ref, k_ref, v_ref, c_ref, s_ref)
    parts = []
    for start, size in cut_blocks(rows):
        stop = start + size + 2 * HALF
        kw, vw = k[start:stop], v[start:stop]
        bias = b_ref[start : start + size, start:stop]
        masks = head_masks(size)
        total = None
        for mask in masks:
            qh = (q[start : start + size] * mask).astype(BF)
            p = soft(qh, kw, bias)
            part = dot(p.astype(BF), vw, NN) * mask
            total = part if total is None else total + part
        parts.append(total)
    o_ref[0] = jnp.concatenate(parts, axis=0).astype(BF)


def bwd_kernel(rows, q_ref, k_ref, v_ref, c_ref, s_ref, b_ref, g_ref, o_ref, acc):
    which = pl.program_id(1)

    @pl.when(which == 0)
    def _():
        q, k, v, cosine, sine = load_qkv(rows, q_ref, k_ref, v_ref, c_ref, s_ref)
        g = g_ref[0].astype(F32)
        acc[...] = jnp.zeros_like(acc)
        for start, size in cut_blocks(rows):
            stop = start + size + 2 * HALF
            kw, vw = k[start:stop], v[start:stop]
            bias = b_ref[start : start + size, start:stop]
            dq = None
            for mask in head_masks(size):
                qh = (q[start : start + size] * mask).astype(BF)
                gh = (g[start : start + size] * mask).astype(BF)
                p = soft(qh, kw, bias)
                dp = dot(gh, vw, NT)
                centre = jnp.sum(p * dp, axis=1, keepdims=True)
                ds = (p * (dp - centre)).astype(BF)
                part = dot(ds, kw, NN) * (mask * (1.0 / math.sqrt(HD)))
                dq = part if dq is None else dq + part
                acc[1, start:stop, :] += dot(ds, qh, TN)
                acc[2, start:stop, :] += dot(p.astype(BF), gh, TN)
            acc[0, HALF + start : HALF + start + size, :] = dq
        for index in range(2):
            w = acc[index]
            acc[index] = w * cosine - swap(w) * sine

    o_ref[0] = acc[which].astype(BF)


def attention_specs(rows, ext, per):
    def column(j):
        return pl.BlockSpec((1, ext, LANES), lambda i, *_: (i // per, 0, j * per + i % per))

    whole = pl.BlockSpec((ext, LANES), lambda *_: (0, 0))
    bias = pl.BlockSpec((rows, ext), lambda *_: (0, 0))
    return [column(0), column(1), column(2), whole, whole, bias]


def attend_fwd(rows, projected, cosine, sine, bias):
    tp, ext, width = projected.shape
    per = width // 3 // LANES
    return pl.pallas_call(
        lambda *refs: fwd_kernel(rows, *refs),
        grid=(tp * per,),
        in_specs=attention_specs(rows, ext, per),
        out_specs=pl.BlockSpec((1, rows, LANES), lambda i: (i // per, 0, i % per)),
        out_shape=jax.ShapeDtypeStruct((tp, rows, width // 3), BF),
        compiler_params=pltpu.CompilerParams(vmem_limit_bytes=32 * 1024 * 1024),
    )(projected, projected, projected, cosine, sine, bias)


def attend_bwd(rows, projected, cosine, sine, bias, grad):
    tp, ext, width = projected.shape
    per = width // 3 // LANES
    specs = attention_specs(rows, ext, per)
    specs.append(pl.BlockSpec((1, rows, LANES), lambda i, j: (i // per, 0, i % per)))
    return pl.pallas_call(
        lambda *refs: bwd_kernel(rows, *refs),
        grid=(tp * per, 3),
        in_specs=specs,
        out_specs=pl.BlockSpec((1, ext, LANES), lambda i, j: (i // per, 0, j * per + i % per)),
        out_shape=jax.ShapeDtypeStruct((tp, ext, width), BF),
        scratch_shapes=[pltpu.VMEM((3, ext, LANES), F32)],
        compiler_params=pltpu.CompilerParams(vmem_limit_bytes=32 * 1024 * 1024),
    )(projected, projected, projected, cosine, sine, bias, grad)


def total_over_all(value):
    for axis in ROWS:
        count, step = lax.axis_size(axis), 1
        while step < count:
            value = value + lax.ppermute(value, axis, [(i, i ^ step) for i in range(count)])
            step *= 2
    return value


def ein(spec, a, b):
    return jnp.einsum(spec, a, b, preferred_element_type=F32)


def body(tokens, lengths, gain_attn, w_qkv, w_out, gain_ffn, w_in, w_down, grad_output):
    rows = tokens.shape[0]
    dp, tp = lax.axis_size("dp"), lax.axis_size("tensor")
    devices = dp * tp
    total = rows * devices
    ext = rows + 2 * HALF
    deep = D // dp
    first = lax.axis_index("dp") * deep
    heads_width, units = w_qkv.shape[2], w_in.shape[2]

    piece = jnp.concatenate(
        [
            lax.dynamic_slice_in_dim(w_qkv, first, deep, 0).reshape(deep, 3 * heads_width),
            lax.dynamic_slice_in_dim(w_out, first, deep, 1).T,
            lax.dynamic_slice_in_dim(w_in, first, deep, 0).reshape(deep, 2 * units),
            lax.dynamic_slice_in_dim(w_down, first, deep, 1).T,
        ],
        axis=1,
    )
    gathered = lax.all_gather(piece, PIECES, axis=0, tiled=True).reshape(tp, D, -1)
    edges = [0, 3 * heads_width, 4 * heads_width, 4 * heads_width + 2 * units]
    edges.append(edges[-1] + units)
    all_qkv, all_out, all_in, all_down = (
        gathered[:, :, edges[i] : edges[i + 1]] for i in range(4)
    )

    start = (lax.axis_index("dp") * tp + lax.axis_index("tensor")) * rows
    forward = [(i, i + 1) for i in range(devices - 1)]
    backward = [(i + 1, i) for i in range(devices - 1)]
    x_own = tokens.astype(F32)
    normed_own, norm_pull_one = jax.vjp(layer_norm, x_own, gain_attn)
    normed_low = normed_own.astype(BF)
    normed_ext = jnp.concatenate(
        [
            lax.ppermute(normed_low[rows - HALF :], ROWS, forward),
            normed_low,
            lax.ppermute(normed_low[:HALF], ROWS, backward),
        ],
        axis=0,
    )
    seg_ext, pos_ext = layout(lengths, start - HALF, ext, total)
    cosine, sine = rotary(pos_ext)
    row_ids = jnp.arange(rows, dtype=jnp.int32)[:, None]
    col_ids = jnp.arange(ext, dtype=jnp.int32)[None, :]
    allowed = (jnp.abs(col_ids - HALF - row_ids) <= HALF) & (
        seg_ext[HALF : HALF + rows][:, None] == seg_ext[None, :]
    )
    bias = jnp.where(allowed, 0.0, -1e30).astype(F32)

    projected = ein("nd,tdk->tnk", normed_ext, all_qkv)
    mixed = attend_fwd(rows, projected, cosine, sine, bias)
    residual = x_own + ein("tnc,tdc->nd", mixed, all_out)
    normed_ffn, norm_pull_two = jax.vjp(layer_norm, residual, gain_ffn)
    normed_ffn_low = normed_ffn.astype(BF)
    hidden = ein("nd,tdk->tnk", normed_ffn_low, all_in)

    def gelu_product(values):
        return jax.nn.gelu(values[..., :units], approximate=False) * values[..., units:]

    activated, gelu_pull = jax.vjp(gelu_product, hidden)
    act_low = activated.astype(BF)
    output = (residual + ein("tnf,tdf->nd", act_low, all_down)).astype(BF)

    grad_out32 = grad_output.astype(F32)
    grad_act = ein("nd,tdf->tnf", grad_output, all_down)
    grad_hidden = gelu_pull(grad_act)[0].astype(BF)
    grad_down = ein("nd,tnf->tdf", grad_output, act_low).astype(BF)
    grad_in = ein("nd,tnk->tdk", normed_ffn_low, grad_hidden).astype(BF)
    ffn_sum = lax.psum_scatter(
        jnp.concatenate([grad_in, grad_down], axis=2).reshape(tp * D, 3 * units),
        PIECES,
        scatter_dimension=0,
        tiled=True,
    )
    grad_normed_ffn = ein("tnk,tdk->nd", grad_hidden, all_in)
    grad_resid_part, grad_gain_two = norm_pull_two(grad_normed_ffn)
    grad_residual = grad_out32 + grad_resid_part
    grad_res_low = grad_residual.astype(BF)
    grad_mixed = ein("nd,tdc->tnc", grad_res_low, all_out).astype(BF)
    grad_wout = ein("nd,tnc->tdc", grad_res_low, mixed).astype(BF)
    grad_qkv_low = attend_bwd(rows, projected, cosine, sine, bias, grad_mixed)
    grad_wqkv = ein("nd,tnk->tdk", normed_ext, grad_qkv_low).astype(BF)
    attn_sum = lax.psum_scatter(
        jnp.concatenate([grad_wqkv, grad_wout], axis=2).reshape(tp * D, 4 * heads_width),
        PIECES,
        scatter_dimension=0,
        tiled=True,
    )
    grad_normed_ext = ein("tnk,tdk->nd", grad_qkv_low, all_qkv)
    from_after = lax.ppermute(grad_normed_ext[:HALF].astype(BF), ROWS, backward)
    from_before = lax.ppermute(grad_normed_ext[ext - HALF :].astype(BF), ROWS, forward)
    grad_normed = (
        grad_normed_ext[HALF : HALF + rows]
        + jnp.pad(from_before.astype(F32), ((0, rows - HALF), (0, 0)))
        + jnp.pad(from_after.astype(F32), ((rows - HALF, 0), (0, 0)))
    )
    grad_x_part, grad_gain_one = norm_pull_one(grad_normed)
    grad_tokens = (grad_residual + grad_x_part).astype(BF)
    gains = total_over_all(jnp.stack([grad_gain_one, grad_gain_two]))

    ffn_sum = ffn_sum.astype(F32)
    attn_sum = attn_sum.astype(F32)
    return (
        output,
        grad_tokens,
        gains[0],
        attn_sum[:, : 3 * heads_width].reshape(deep, 3, heads_width),
        attn_sum[:, 3 * heads_width :].T,
        gains[1],
        ffn_sum[:, : 2 * units].reshape(deep, 2, units),
        ffn_sum[:, 2 * units :].T,
    )


def solution(mesh):
    in_specs = (
        P(("dp", "tensor"), None),
        P(),
        P(),
        P(None, None, "tensor"),
        P("tensor", None),
        P(),
        P(None, None, "tensor"),
        P("tensor", None),
        P(("dp", "tensor"), None),
    )
    out_specs = (
        P(("dp", "tensor"), None),
        P(("dp", "tensor"), None),
        P(),
        P("dp", None, "tensor"),
        P("tensor", "dp"),
        P(),
        P("dp", None, "tensor"),
        P("tensor", "dp"),
    )
    return jax.shard_map(body, mesh=mesh, in_specs=in_specs, out_specs=out_specs, check_vma=False)
```

time: 1040 us -> 697 us (0.67)
  waiting for transfers between devices: 627 us -> 395 us
  matrix products: 155 us -> 96.8 us
  Pallas kernels: 0 us -> 46.3 us
  blocking collectives: 40.5 us -> 0 us
  local copies, waits for them, and re-layouts: 114 us -> 86.2 us
  other arithmetic: 64.9 us -> 37.5 us
    reduce_scatter x8 -> x2, waiting for transfers between devices: 368 us -> 226 us  [the longest x1 178 us: body(): lax.psum_scatter(jnp.concatenate([grad_in, grad_down], axis=2).reshape(tp...]
    all_gather x4 -> x1, waiting for transfers between devices: 257 us -> 148 us  [body(): lax.all_gather(piece, PIECES, axis=0, tiled=True).reshape(tp, D, -1)]
    dynamic_update_slice x12 -> x0, local copies, waits for them, and re-layouts: 65.2 us -> none  [the longest x6 42.4 us: body(): lax.scan(attend_backward, (zeros_ext, zeros_ext), jnp.arange(blocks_num,...]
    dot_general x33 -> x12, matrix products: 155 us -> 96.8 us  [ein(): return jnp.einsum(spec, a, b, preferred_element_type=F32)]
    pallas_call x0 -> x2, Pallas kernels: none -> 46.3 us  [the longest x1 31.2 us: attend_bwd(): pl.pallas_call(lambda *refs: bwd_kernel(rows, *refs), grid=(tp * per, 3),...]
    psum x1 -> x0, blocking collectives: 40.5 us -> none  [body(): lax.psum((grad_gain_one, grad_gain_two), ('dp', 'tensor'))]
    all_gather x0 -> x1, local copies, waits for them, and re-layouts: none -> 32.7 us  [body(): lax.all_gather(piece, PIECES, axis=0, tiled=True).reshape(tp, D, -1)]
    concatenate x1 -> x2, local copies, waits for them, and re-layouts: 4.37 us -> 33.2 us  [the longest x1 21.9 us: body(): jnp.concatenate([grad_in, grad_down], axis=2).reshape(tp * D, 3 * units)]
  transfers between devices with their start and end apart: 16 -> 12, of which waited for: 13 -> 9; matrix products, arithmetic and copies ran while one was open for 6% -> 16% of each run, Pallas kernels for 0% -> 0%
where the time goes in v1:
time: 697 us; the launch traced here: 690 us
  waiting for transfers between devices  395 us (57%)
  matrix products  96.8 us (14%)
  local copies, waits for them, and re-layouts  86.2 us (12%)
  Pallas kernels  46.3 us (7%)
  other arithmetic  37.5 us (5%)
  between operations  14.5 us (2%)
  starting transfers between devices  13.9 us (2%)
    reduce_scatter x1, waiting for transfers between devices, body(): lax.psum_scatter(jnp.concatenate([grad_in, grad_down], axis=2).reshape(tp...  178 us
    all_gather x1, waiting for transfers between devices, body(): lax.all_gather(piece, PIECES, axis=0, tiled=True).reshape(tp, D, -1)  148 us
    dot_general x12, matrix products, ein(): return jnp.einsum(spec, a, b, preferred_element_type=F32)  96.8 us
    reduce_scatter x1, waiting for transfers between devices, body(): lax.psum_scatter(jnp.concatenate([grad_wqkv, grad_wout], axis=2).reshape(...  48.2 us
    all_gather x1, local copies, waits for them, and re-layouts, body(): lax.all_gather(piece, PIECES, axis=0, tiled=True).reshape(tp, D, -1)  32.7 us
    pallas_call x1, Pallas kernels, attend_bwd(): pl.pallas_call(lambda *refs: bwd_kernel(rows, *refs), grid=(tp * per, 3),...  31.2 us
    concatenate x1, local copies, waits for them, and re-layouts, body(): jnp.concatenate([grad_in, grad_down], axis=2).reshape(tp * D, 3 * units)  21.9 us
    pallas_call x1, Pallas kernels, attend_fwd(): pl.pallas_call(lambda *refs: fwd_kernel(rows, *refs), grid=(tp * per,), i...  15.1 us
  transfers between devices with their start and end apart: 12, of which 9 were waited for; matrix products, arithmetic and copies ran while one was open for 16% of the time, Pallas kernels for 0%

profile of v1, /device:TPU:0, one launch (start us, length us, event | category | flops | bytes accessed | tf_op | source)
XLA Modules:
  0.0 690.5 jit_solution(1103302362850972361)
XLA Ops:
  7.3 1.6 dynamic-slice_bitcast_fusion.1
  8.9 1.6 dynamic-slice_bitcast_fusion
  10.5 1.6 constant_dynamic-slice_fusion.1
  12.1 1.7 copy.85
  13.9 2.0 pad_maximum_fusion.2
  16.0 1.3 convert_reduce_fusion
  19.9 5.6 collective-permute-start
  25.5 1.3 collective-permute-start.1
  27.6 1.0 fusion.63
  29.1 148.4 %all-gather.2.cloned.1.call-done = bf16[4096,2992]{0,1:T(8,128)(2,1)} async-done(((bf16[128,2992]{0,1:T(8,128)(2,1)}), bf16[4096,2992]{0,1:T(8,128)(2,1)}) %all-gather.2.cloned.1.call-update) | async-done | bytes 24510480 | tf_op jit(solution)/shard_map/all_gather | solution.py:212
  177.6 32.7 %copy.67 = bf16[4096,2992]{1,0:T(8,128)(2,1)} copy(bf16[4096,2992]{0,1:T(8,128)(2,1)} %all-gather.2.cloned.1.call-done) | data formatting | bytes 49020928 | tf_op jit(solution)/shard_map/all_gather | solution.py:212
  210.3 5.8 fusion.23.refs_0_.refs_1_.refs_2_
  216.1 15.1 %shard_map.152 = bf16[4,408,256]{2,1,0:T(8,128)(2,1)S(1)} custom-call(f32[4,536,768]{2,1,0:T(8,128)S(1)} %fusion.23.refs_0_.refs_1_.refs_2_, f32[4,536,768]{2,1,0:T(8,128)S(1)} %fusion.23.refs_0_.refs_1_.refs_2_, f32[4,536,768]{2,1,0:T(8,128)S(1)} %fusion.23.refs_0_.refs_1_.refs_2_, f32[536,128]{1,0:T(8,128)S(1)} %get-tuple-element.69.refs_3_, ...), custom_call_target="tpu_custom_call" | custom-call | tf_op jit(solution)/shard_map/pallas_call | solution.py:154
  231.2 2.8 fusion.85
  234.3 8.4 %fusion.5 = f32[4,408,1312]{2,1,0:T(8,128)S(1)} fusion(bf16[4,1024,2992]{2,1,0:T(8,128)(2,1)} %bitcast.88, f32[408,1024]{1,0:T(8,128)S(1)} %get-tuple-element.64, f32[1024]{0:T(1024)S(1)} %copy-done.27, f32[408]{0:T(512)S(1)} %fusion.71, f32[408]{0:T(512)S(1)} %broadcast_multiply_fusion), kind=kOutput, calls=%fused_computation.11 | convolution fusion | flops 4386816000 | bytes 21777600 | tf_op jit(solution)/shard_map/nd,tdk->tnk/dot_general | solution.py:190
  242.7 16.3 %bitcast_multiply_fusion.1 = (f32[4,408,656]{2,1,0:T(8,128)}, f32[4,408,656]{2,1,0:T(8,128)S(1)}, f32[4,656,408]{1,2,0:T(8,128)}) fusion(f32[4,408,1312]{2,1,0:T(8,128)S(1)} %fusion.5, bf16[408,1024]{1,0:T(8,128)(2,1)S(1)} %copy-done.12, bf16[4,1024,2992]{2,1,0:T(8,128)(2,1)} %bitcast.89), kind=kOutput, calls=%fused_computation.23 | convolution fusion | flops 2262160896 | bytes 24256512 | tf_op jit(solution)/shard_map/nd,tdf->tnf/dot_general | solution.py:190
  259.0 6.8 multiply_add_fusion
  265.8 13.9 %fusion.41 = (f32[1024]{0:T(1024)S(1)}, f32[408]{0:T(512)S(1)}, f32[408,1024,1]{1,0,2:T(8,128)}) fusion(f32[408,1024]{1,0:T(8,128)} %copy-done.9, f32[408]{0:T(512)S(1)} %fusion.71, f32[408]{0:T(512)S(1)} %broadcast_multiply_fusion, f32[1024]{0:T(1024)S(1)} %copy-done.27, bf16[4,1024,2992]{2,1,0:T(8,128)(2,1)} %bitcast.90, ...), kind=kOutput, calls=%fused_computation.66 | convolution fusion | flops 4392350208 | bytes 24916768 | tf_op jit(solution)/shard_map/tnk,tdk->nd/dot_general | solution.py:190
  279.8 2.5 fusion.80
  282.6 3.4 fusion.53.refs_6_
  286.0 2.7 convert_bitcast_fusion.2
  288.7 31.2 %shard_map.153 = bf16[4,536,768]{2,1,0:T(8,128)(2,1)S(1)} custom-call(f32[4,536,768]{2,1,0:T(8,128)S(1)} %bitcast.83, f32[4,536,768]{2,1,0:T(8,128)S(1)} %bitcast.83, f32[4,536,768]{2,1,0:T(8,128)S(1)} %bitcast.83, f32[536,128]{1,0:T(8,128)S(1)} %get-tuple-element.69.refs_3_, f32[536,128]{1,0:T(8,128)S(1)} %get-tuple-element.70.refs_4_, ...), custom_call_target="tpu_custom_call" | custom-call | tf_op jit(solution)/shard_map/pallas_call | solution.py:169
  319.9 1.7 copy-done.3
  321.7 8.8 %convert_bitcast_fusion = bf16[4,1024,768]{1,2,0:T(8,128)(2,1)} fusion(bf16[4,536,768]{2,1,0:T(8,128)(2,1)S(1)} %shard_map.153, bf16[64,1024]{1,0:T(8,128)(2,1)} %collective-permute-done.1, bf16[408,1024]{1,0:T(8,128)(2,1)S(1)} %copy-done.18, bf16[64,1024]{1,0:T(8,128)(2,1)} %collective-permute-done), kind=kOutput, calls=%fused_computation.10 | convolution fusion | flops 3378659328 | bytes 10682368 | tf_op jit(solution)/shard_map/nd,tnk->tdk/dot_general | solution.py:190
  330.4 7.0 %pad_maximum_fusion.1 = bf16[4,1024,1024]{1,2,0:T(8,128)(2,1)} fusion(bf16[4,1024,256]{1,2,0:T(8,128)(2,1)S(1)} %copy-done.16, bf16[4,1024,768]{1,2,0:T(8,128)(2,1)} %convert_bitcast_fusion), kind=kLoop, calls=%fused_computation.8 | loop fusion | flops 16777216 | bytes 16777216 | tf_op jit(solution)/shard_map/concatenate | solution.py:276
  337.4 11.4 %copy.74 = bf16[4,1024,1024]{2,1,0:T(8,128)(2,1)} copy(bf16[4,1024,1024]{1,2,0:T(8,128)(2,1)} %pad_maximum_fusion.1) | data formatting | bytes 16777216 | tf_op jit(solution)/shard_map/concatenate | solution.py:276
  348.9 1.1 copy-done.13
  350.0 6.9 %convert_bitcast_fusion.1 = bf16[4,1024,656]{1,2,0:T(8,128)(2,1)} fusion(bf16[4,408,656]{2,1,0:T(8,128)(2,1)} %get-tuple-element.53, bf16[408,1024]{1,0:T(8,128)(2,1)S(1)} %copy-done.13), kind=kOutput, calls=%fused_computation.20 | convolution fusion | flops 2195259392 | bytes 8350720 | tf_op jit(solution)/shard_map/nd,tnf->tdf/dot_general | solution.py:190
  356.9 15.1 %fusion = bf16[4,1024,1312]{1,2,0:T(8,128)(2,1)S(1)} fusion(f32[4,408,656]{2,1,0:T(8,128)} %get-tuple-element.52, f32[4,408,656]{2,1,0:T(8,128)} %get-tuple-element.50, f32[408,1024]{1,0:T(8,128)S(1)} %copy-done.10, f32[1024]{0:T(1024)S(1)} %copy-done.27, f32[408]{0:T(512)S(1)} %fusion.71, f32[408]{0:T(512)S(1)} %broadcast_multiply_fusion), kind=kOutput, calls=%fused_computation.2 | convolution fusion | flops 4396472320 | bytes 20991168 | tf_op jit(solution)/shard_map/nd,tnk->tdk/dot_general | solution.py:190
  372.0 9.7 %pad_maximum_fusion = bf16[4,1024,1968]{1,2,0:T(8,128)(2,1)} fusion(bf16[4,1024,656]{1,2,0:T(8,128)(2,1)} %convert_bitcast_fusion.1, bf16[4,1024,1312]{1,2,0:T(8,128)(2,1)S(1)} %fusion), kind=kLoop, calls=%fused_computation | loop fusion | flops 32243712 | bytes 32243712 | tf_op jit(solution)/shard_map/concatenate | solution.py:262
  381.7 21.9 %copy.76 = bf16[4,1024,1968]{2,1,0:T(8,128)(2,1)} copy(bf16[4,1024,1968]{1,2,0:T(8,128)(2,1)} %pad_maximum_fusion) | data formatting | bytes 32243712 | tf_op jit(solution)/shard_map/concatenate | solution.py:262
  403.6 1.9 copy-done.4
  405.6 6.0 fusion.86
  411.6 3.0 collective-permute-start.2
  414.6 1.5 collective-permute-start.3
  416.1 3.3 collective-permute-done.2
  419.4 6.2 collective-permute-done.3
  426.5 6.9 fusion.42
  433.5 3.6 collective-permute-done.5
  437.8 3.0 collective-permute-done.6
  441.5 3.0 collective-permute-done.7
  444.5 1.6 collective-permute-start.8
  446.2 1.3 add_convert_fusion.1
  447.5 1.6 collective-permute-done.8
  449.7 48.2 %reduce-scatter.3.cloned.1.call-done = bf16[128,1024]{1,0:T(8,128)(2,1)} async-done(((bf16[4096,1024]{1,0:T(8,128)(2,1)}), bf16[128,1024]{1,0:T(8,128)(2,1)}) %reduce-scatter.3.cloned.1.call-update) | async-done | bytes 262160 | tf_op jit(solution)/shard_map/reduce_scatter | solution.py:275
  501.7 177.7 %reduce-scatter.5.cloned.1.call-done = bf16[128,1968]{1,0:T(8,128)(2,1)} async-done(((bf16[4096,1968]{1,0:T(8,128)(2,1)}), bf16[128,1968]{1,0:T(8,128)(2,1)}) %reduce-scatter.5.cloned.1.call-update) | async-done | bytes 503824 | tf_op jit(solution)/shard_map/reduce_scatter | solution.py:261
  680.5 1.1 copy.77
  681.5 1.1 convert_element_type.102
  (117 shorter events, 13.5 us)
Async XLA Ops:
  7.2 6.7 copy-start
  7.2 10.1 %copy-start.5 = (bf16[408,1024]{1,0:T(8,128)(2,1)S(1)}, bf16[408,1024]{1,0:T(8,128)(2,1)}, u32[]{:S(2)}) copy-start(bf16[408,1024]{1,0:T(8,128)(2,1)} %param.9) | copy-start | bytes 2506756
  7.2 11.7 %copy-start.21 = (f32[1024]{0:T(1024)S(1)}, f32[1024]{0:T(1024)}, u32[]{:S(2)}) copy-start(f32[1024]{0:T(1024)} %param.11) | copy-start | bytes 12292
  7.2 19.6 %copy-start.28 = (s32[25]{0:T(128)S(1)}, s32[25]{0:T(128)}, u32[]{:S(2)}) copy-start(s32[25]{0:T(128)} %param.10) | copy-start | bytes 304
  7.2 170.4 %all-gather.2.cloned.1.call-start = ((), (), s32[]{:S(2)}) async-start(), calls=%async_computation.2 | async-start | bytes 25276416 | tf_op jit(solution)/shard_map/all_gather | solution.py:212
  15.9 481.9 %reduce-scatter.3.cloned.1.call-start = ((), (), s32[]{:S(2)}) async-start(), calls=%async_computation.3 | async-start | bytes 8650752 | tf_op jit(solution)/shard_map/reduce_scatter | solution.py:275
  17.3 0.6 copy-start.19
  17.7 0.6 copy-start.25
  18.3 0.6 copy-start.23
  19.2 191.1 %copy-start.17 = (bf16[408,1024]{1,0:T(8,128)(2,1)}, bf16[408,1024]{1,0:T(8,128)(2,1)S(1)}, u32[]{:S(2)}) copy-start(bf16[408,1024]{1,0:T(8,128)(2,1)S(1)} %fusion.36) | copy-start | bytes 2506756
  19.9 190.3 %collective-permute-start = (bf16[64,1024]{1,0:T(8,128)(2,1)}, bf16[64,1024]{1,0:T(8,128)(2,1)}, u32[]{:S(2)}, u32[]{:S(2)}) collective-permute-start(bf16[64,1024]{1,0:T(8,128)(2,1)} %get-tuple-element.56), channel_id=1, source_target_pairs={{0,1},{1,2},{2,3},{3,4},{4,5},{5,6},{6,7},{7,8},{8,9},{9,10},{10,1... | collective-permute-start | bytes 393224 | tf_op jit(solution)/shard_map/ppermute | solution.py:227
  25.5 184.8 %collective-permute-start.1 = (bf16[64,1024]{1,0:T(8,128)(2,1)S(1)}, bf16[64,1024]{1,0:T(8,128)(2,1)}, u32[]{:S(2)}, u32[]{:S(2)}) collective-permute-start(bf16[64,1024]{1,0:T(8,128)(2,1)S(1)} %get-tuple-element.57), channel_id=1, source_target_pairs={{1,0},{2,1},{3,2},{4,3},{5,4},{6,5},{7,6},{8,7},{9,8},{10,9},{11,1... | collective-permute-start | bytes 393224 | tf_op jit(solution)/shard_map/ppermute | solution.py:229
  216.1 15.1 %copy-start.2 = (f32[4,536,768]{2,1,0:T(8,128)}, f32[4,536,768]{2,1,0:T(8,128)S(1)}, u32[]{:S(2)}) copy-start(f32[4,536,768]{2,1,0:T(8,128)S(1)} %fusion.23.refs_0_.refs_1_.refs_2_) | copy-start | bytes 19759108
  231.2 3.1 copy-start.27
  233.9 8.7 %copy-start.9 = (f32[408,1024]{1,0:T(8,128)}, f32[408,1024]{1,0:T(8,128)S(1)}, u32[]{:S(2)}) copy-start(f32[408,1024]{1,0:T(8,128)S(1)} %get-tuple-element.64) | copy-start | bytes 5013508
  234.3 8.4 %copy-start.12 = (bf16[408,1024]{1,0:T(8,128)(2,1)S(1)}, bf16[408,1024]{1,0:T(8,128)(2,1)}, u32[]{:S(2)}) copy-start(bf16[408,1024]{1,0:T(8,128)(2,1)} %param.17) | copy-start | bytes 2506756
  282.3 3.7 copy-start.7
  282.3 6.4 slice-start
  282.6 6.1 slice-start.1
  288.7 33.0 %copy-start.18 = (bf16[408,1024]{1,0:T(8,128)(2,1)S(1)}, bf16[408,1024]{1,0:T(8,128)(2,1)}, u32[]{:S(2)}) copy-start(bf16[408,1024]{1,0:T(8,128)(2,1)} %copy-done.17) | copy-start | bytes 2506756
  319.9 1.7 copy-start.3
  321.7 8.8 %copy-start.16 = (bf16[4,1024,256]{1,2,0:T(8,128)(2,1)S(1)}, bf16[4,1024,256]{1,2,0:T(8,128)(2,1)}, u32[]{:S(2)}) copy-start(bf16[4,1024,256]{1,2,0:T(8,128)(2,1)} %convert_bitcast_fusion.2) | copy-start | bytes 6291460
  348.8 1.1 copy-start.13
  348.8 330.6 %reduce-scatter.5.cloned.1.call-start = ((), (), s32[]{:S(2)}) async-start(), calls=%async_computation.4 | async-start | bytes 17301504 | tf_op jit(solution)/shard_map/reduce_scatter | solution.py:261
  350.0 6.9 %copy-start.10 = (f32[408,1024]{1,0:T(8,128)S(1)}, f32[408,1024]{1,0:T(8,128)}, u32[]{:S(2)}) copy-start(f32[408,1024]{1,0:T(8,128)} %copy-done.9) | copy-start | bytes 5013508
  403.6 1.9 copy-start.4
  405.6 20.1 %copy-start.6 = (bf16[408,1024]{1,0:T(8,128)(2,1)S(1)}, bf16[408,1024]{1,0:T(8,128)(2,1)}, u32[]{:S(2)}) copy-start(bf16[408,1024]{1,0:T(8,128)(2,1)} %param.9) | copy-start | bytes 2506756
  405.6 20.1 %copy-start.20 = (f32[408]{0:T(512)S(1)}, f32[408]{0:T(512)}, u32[]{:S(2)}) copy-start(f32[408]{0:T(512)} %copy-done.19) | copy-start | bytes 4900
  405.6 20.1 %copy-start.22 = (f32[1024]{0:T(1024)S(1)}, f32[1024]{0:T(1024)}, u32[]{:S(2)}) copy-start(f32[1024]{0:T(1024)} %param.11) | copy-start | bytes 12292
  405.6 20.1 %copy-start.24 = (f32[408]{0:T(512)S(1)}, f32[408]{0:T(512)}, u32[]{:S(2)}) copy-start(f32[408]{0:T(512)} %copy-done.23) | copy-start | bytes 4900
  405.6 20.9 %copy-start.11 = (f32[408,1024]{1,0:T(8,128)S(1)}, f32[408,1024]{1,0:T(8,128)}, u32[]{:S(2)}) copy-start(f32[408,1024]{1,0:T(8,128)} %copy-done.9) | copy-start | bytes 5013508
  405.6 20.9 %copy-start.15 = (bf16[4,408,656]{2,1,0:T(8,128)(2,1)S(1)}, bf16[4,408,656]{2,1,0:T(8,128)(2,1)}, u32[]{:S(2)}) copy-start(bf16[4,408,656]{2,1,0:T(8,128)(2,1)} %get-tuple-element.53) | copy-start | bytes 6423556
  411.6 7.8 %collective-permute-start.2 = (bf16[64,1024]{1,0:T(8,128)(2,1)S(1)}, bf16[64,1024]{1,0:T(8,128)(2,1)S(1)}, u32[]{:S(2)}, u32[]{:S(2)}) collective-permute-start(bf16[64,1024]{1,0:T(8,128)(2,1)S(1)} %get-tuple-element.54), channel_id=1, source_target_pairs={{0,1},{1,2},{2,3},{3,4},{4,5},{5,6},{6,7},{7,8},{8,9},{9,10},{10,1... | collective-permute-start | bytes 393224 | tf_op jit(solution)/shard_map/ppermute | solution.py:283
  414.6 11.1 %collective-permute-start.3 = (bf16[64,1024]{1,0:T(8,128)(2,1)S(1)}, bf16[64,1024]{1,0:T(8,128)(2,1)S(1)}, u32[]{:S(2)}, u32[]{:S(2)}) collective-permute-start(bf16[64,1024]{1,0:T(8,128)(2,1)S(1)} %get-tuple-element.55), channel_id=1, source_target_pairs={{1,0},{2,1},{3,2},{4,3},{5,4},{6,5},{7,6},{8,7},{9,8},{10,9},{11,1... | collective-permute-start | bytes 393224 | tf_op jit(solution)/shard_map/ppermute | solution.py:282
  426.3 7.1 %copy-start.26 = (f32[408]{0:T(512)S(1)}, f32[408]{0:T(512)}, u32[]{:S(2)}) copy-start(f32[408]{0:T(512)} %copy-done.25) | copy-start | bytes 4900
  426.4 7.0 %collective-permute-start.4 = (f32[2,1024]{1,0:T(2,128)S(1)}, f32[2,1024]{1,0:T(2,128)S(1)}, u32[]{:S(2)}, u32[]{:S(2)}) collective-permute-start(f32[2,1024]{1,0:T(2,128)S(1)} %pad_maximum_fusion.5), channel_id=1, source_target_pairs={{0,4},{4,0},{8,12},{12,8},{16,20},{20,16},{24,28},{28,24},{1,5},{5... | collective-permute-start | bytes 24584 | tf_op jit(solution)/shard_map/ppermute | solution.py:184
  433.3 12.8 %copy-start.8 = (f32[408,1024]{1,0:T(8,128)S(1)}, f32[408,1024]{1,0:T(8,128)}, u32[]{:S(2)}) copy-start(f32[408,1024]{1,0:T(8,128)} %copy-done.7) | copy-start | bytes 5013508
  433.3 12.8 %copy-start.14 = (bf16[408,1024]{1,0:T(8,128)(2,1)S(1)}, bf16[408,1024]{1,0:T(8,128)(2,1)}, u32[]{:S(2)}) copy-start(bf16[408,1024]{1,0:T(8,128)(2,1)} %param.17) | copy-start | bytes 2506756
  433.4 3.7 collective-permute-start.5
  437.1 3.8 collective-permute-start.6
  440.9 3.7 collective-permute-start.7
  444.5 4.6 collective-permute-start.8
  446.2 237.6 %copy-start.1 = (bf16[1024,2,656]{0,2,1:T(8,128)(2,1)S(1)}, bf16[1024,2,656]{0,2,1:T(8,128)(2,1)}, u32[]{:S(2)}) copy-start(bf16[1024,2,656]{0,2,1:T(8,128)(2,1)} %param.15) | copy-start | bytes 8060932
Sparse Core Ops, SparseCore 0:
  16.1 161.4 all-gather.1
  349.0 148.8 reduce-scatter.2
  500.2 179.2 reduce-scatter.4

commit v2 on v1

--- a/solution.py
+++ b/solution.py
@@ -5,6 +5,7 @@
 from jax import lax
 from jax.experimental import pallas as pl
 from jax.experimental.pallas import tpu as pltpu
+from jax.experimental.layout import Layout, with_layout_constraint
 from jax.sharding import PartitionSpec as P
 
 D = 1024
@@ -177,6 +178,37 @@
     )(projected, projected, projected, cosine, sine, bias, grad)
 
 
+def pair_kernel(l1_ref, r1_ref, l2_ref, r2_ref, o_ref):
+    width = r1_ref.shape[2]
+    o_ref[:, :width] = dot(l1_ref[...], r1_ref[0], TN).astype(BF)
+    o_ref[:, width:] = dot(l2_ref[...], r2_ref[0], TN).astype(BF)
+
+
+def pair_products(l1, r1, l2, r2):
+    tp, n1, k1 = r1.shape
+    n2, k2 = r2.shape[1:]
+    deep = l1.shape[1]
+    tile = 2 * LANES
+    count = deep // tile
+    return pl.pallas_call(
+        pair_kernel,
+        grid=(tp, count),
+        in_specs=[
+            pl.BlockSpec((n1, tile), lambda t, j: (0, j)),
+            pl.BlockSpec((1, n1, k1), lambda t, j: (t, 0, 0)),
+            pl.BlockSpec((n2, tile), lambda t, j: (0, j)),
+            pl.BlockSpec((1, n2, k2), lambda t, j: (t, 0, 0)),
+        ],
+        out_specs=pl.BlockSpec((tile, k1 + k2), lambda t, j: (t * count + j, 0)),
+        out_shape=jax.ShapeDtypeStruct((tp * deep, k1 + k2), BF),
+        compiler_params=pltpu.CompilerParams(vmem_limit_bytes=32 * 1024 * 1024),
+    )(l1, r1, l2, r2)
+
+
+def padded(block):
+    return jnp.pad(block, ((0, 0), (0, -block.shape[1] % LANES)))
+
+
 def total_over_all(value):
     for axis in ROWS:
         count, step = lax.axis_size(axis), 1
@@ -200,21 +232,20 @@
     first = lax.axis_index("dp") * deep
     heads_width, units = w_qkv.shape[2], w_in.shape[2]
 
-    piece = jnp.concatenate(
-        [
-            lax.dynamic_slice_in_dim(w_qkv, first, deep, 0).reshape(deep, 3 * heads_width),
-            lax.dynamic_slice_in_dim(w_out, first, deep, 1).T,
-            lax.dynamic_slice_in_dim(w_in, first, deep, 0).reshape(deep, 2 * units),
-            lax.dynamic_slice_in_dim(w_down, first, deep, 1).T,
-        ],
-        axis=1,
-    )
-    gathered = lax.all_gather(piece, PIECES, axis=0, tiled=True).reshape(tp, D, -1)
-    edges = [0, 3 * heads_width, 4 * heads_width, 4 * heads_width + 2 * units]
-    edges.append(edges[-1] + units)
-    all_qkv, all_out, all_in, all_down = (
-        gathered[:, :, edges[i] : edges[i + 1]] for i in range(4)
-    )
+    blocks = [
+        lax.dynamic_slice_in_dim(w_qkv, first, deep, 0).reshape(deep, 3 * heads_width),
+        lax.dynamic_slice_in_dim(w_out, first, deep, 1).T,
+        lax.dynamic_slice_in_dim(w_in, first, deep, 0).reshape(deep, 2 * units),
+        lax.dynamic_slice_in_dim(w_down, first, deep, 1).T,
+    ]
+    piece = jnp.concatenate([padded(block) for block in blocks], axis=1)
+    gathered = lax.all_gather(piece, PIECES, axis=0, tiled=True)
+    gathered = with_layout_constraint(gathered, Layout((0, 1))).reshape(tp, D, -1)
+    weights, offset = [], 0
+    for block in blocks:
+        weights.append(gathered[:, :, offset : offset + block.shape[1]])
+        offset += block.shape[1] + -block.shape[1] % LANES
+    all_qkv, all_out, all_in, all_down = weights
 
     start = (lax.axis_index("dp") * tp + lax.axis_index("tensor")) * rows
     forward = [(i, i + 1) for i in range(devices - 1)]
@@ -256,10 +287,10 @@
     grad_out32 = grad_output.astype(F32)
     grad_act = ein("nd,tdf->tnf", grad_output, all_down)
     grad_hidden = gelu_pull(grad_act)[0].astype(BF)
-    grad_down = ein("nd,tnf->tdf", grad_output, act_low).astype(BF)
-    grad_in = ein("nd,tnk->tdk", normed_ffn_low, grad_hidden).astype(BF)
+    ffn_terms = pair_products(normed_ffn_low, grad_hidden, grad_output, act_low)
+    ffn_terms, grad_hidden = lax.optimization_barrier((ffn_terms, grad_hidden))
     ffn_sum = lax.psum_scatter(
-        jnp.concatenate([grad_in, grad_down], axis=2).reshape(tp * D, 3 * units),
+        ffn_terms,
         PIECES,
         scatter_dimension=0,
         tiled=True,
@@ -269,11 +300,11 @@
     grad_residual = grad_out32 + grad_resid_part
     grad_res_low = grad_residual.astype(BF)
     grad_mixed = ein("nd,tdc->tnc", grad_res_low, all_out).astype(BF)
-    grad_wout = ein("nd,tnc->tdc", grad_res_low, mixed).astype(BF)
     grad_qkv_low = attend_bwd(rows, projected, cosine, sine, bias, grad_mixed)
-    grad_wqkv = ein("nd,tnk->tdk", normed_ext, grad_qkv_low).astype(BF)
+    attn_terms = pair_products(normed_ext, grad_qkv_low, grad_res_low, mixed)
+    attn_terms, ffn_sum = lax.optimization_barrier((attn_terms, ffn_sum))
     attn_sum = lax.psum_scatter(
-        jnp.concatenate([grad_wqkv, grad_wout], axis=2).reshape(tp * D, 4 * heads_width),
+        attn_terms,
         PIECES,
         scatter_dimension=0,
         tiled=True,

time: 697 us -> 613 us (0.88)
  local copies, waits for them, and re-layouts: 86.2 us -> 31.8 us
  matrix products: 96.8 us -> 62 us
  Pallas kernels: 46.3 us -> 73.9 us
  other arithmetic: 37.5 us -> 25.2 us
    dot_general x12 -> x8, matrix products: 96.8 us -> 62 us  [ein(): return jnp.einsum(spec, a, b, preferred_element_type=F32)]
    concatenate x2 -> x0, local copies, waits for them, and re-layouts: 33.2 us -> none  [the longest x1 21.9 us: body(): jnp.concatenate([grad_in, grad_down], axis=2).reshape(tp * D, 3 * units)]
    all_gather x1 -> x0, local copies, waits for them, and re-layouts: 32.7 us -> none  [body(): lax.all_gather(piece, PIECES, axis=0, tiled=True).reshape(tp, D, -1)]
    pallas_call x0 -> x2, Pallas kernels: none -> 27.3 us  [pair_products(): pl.pallas_call(pair_kernel, grid=(tp, count), in_specs=[pl.BlockSpec((n1,...]
    concatenate x3 -> x2, other arithmetic: 18.7 us -> 3.97 us  [the longest x1 2.01 us: body(): piece = jnp.concatenate([padded(block) for block in blocks], axis=1)]
    reduce_scatter x2, waiting for transfers between devices: 226 us -> 218 us  [the longest x1 112 us: body(): lax.psum_scatter(ffn_terms, PIECES, scatter_dimension=0, tiled=True)]
    ppermute x1, waiting for transfers between devices: 0.01 us -> 8.36 us  [body(): lax.ppermute(normed_low[:HALF], ROWS, backward)]
    unnamed x66 -> x76, local copies, waits for them, and re-layouts: 10.3 us -> 18.2 us
  transfers between devices with their start and end apart: 12 -> 12, of which waited for: 9 -> 10; matrix products, arithmetic and copies ran while one was open for 16% -> 7% of each run, Pallas kernels for 0% -> 7%
where the time goes in v2:
time: 613 us; the launch traced here: 612 us
  waiting for transfers between devices  391 us (64%)
  Pallas kernels  73.9 us (12%)
  matrix products  62 us (10%)
  local copies, waits for them, and re-layouts  31.8 us (5%)
  other arithmetic  25.2 us (4%)
  between operations  14.4 us (2%)
  starting transfers between devices  14 us (2%)
    all_gather x1, waiting for transfers between devices, body(): gathered = lax.all_gather(piece, PIECES, axis=0, tiled=True)  145 us
    reduce_scatter x1, waiting for transfers between devices, body(): lax.psum_scatter(ffn_terms, PIECES, scatter_dimension=0, tiled=True)  112 us
    reduce_scatter x1, waiting for transfers between devices, body(): lax.psum_scatter(attn_terms, PIECES, scatter_dimension=0, tiled=True)  105 us
    dot_general x8, matrix products, ein(): return jnp.einsum(spec, a, b, preferred_element_type=F32)  62 us
    pallas_call x1, Pallas kernels, attend_bwd(): pl.pallas_call(lambda *refs: bwd_kernel(rows, *refs), grid=(tp * per, 3),...  31.5 us
    pallas_call x2, Pallas kernels, pair_products(): pl.pallas_call(pair_kernel, grid=(tp, count), in_specs=[pl.BlockSpec((n1,...  27.3 us
    unnamed x76, local copies, waits for them, and re-layouts  18.2 us
    pallas_call x1, Pallas kernels, attend_fwd(): pl.pallas_call(lambda *refs: fwd_kernel(rows, *refs), grid=(tp * per,), i...  15.1 us
  transfers between devices with their start and end apart: 12, of which 10 were waited for; matrix products, arithmetic and copies ran while one was open for 7% of the time, Pallas kernels for 7%

profile of v2, /device:TPU:0, one launch (start us, length us, event | category | flops | bytes accessed | tf_op | source)
XLA Modules:
  0.0 612.3 jit_solution(1755077418491633730)
XLA Ops:
  7.3 1.6 constant_dynamic-slice_fusion.2
  8.9 1.6 copy.81
  10.5 1.6 constant_dynamic-slice_fusion
  12.1 1.7 copy.82
  13.8 1.6 constant_dynamic-slice_fusion.3
  15.4 1.7 copy.80
  17.2 1.7 copy.64
  19.7 1.2 copy.62
  20.9 2.0 fusion.66
  24.7 4.9 collective-permute-start
  29.6 1.3 collective-permute-start.1
  33.3 8.4 %collective-permute-done.1 = bf16[64,1024]{1,0:T(8,128)(2,1)} collective-permute-done((bf16[64,1024]{1,0:T(8,128)(2,1)}, bf16[64,1024]{1,0:T(8,128)(2,1)}, u32[]{:S(2)}, u32[]{:S(2)}) %collective-permute-start.1) | collective-permute-done | bytes 131104 | tf_op jit(solution)/shard_map/ppermute | solution.py:260
  41.6 145.1 %all-gather.2.cloned.1.call-done = bf16[4096,3200]{1,0:T(8,128)(2,1)} async-done(((bf16[128,3200]{1,0:T(8,128)(2,1)}), bf16[4096,3200]{1,0:T(8,128)(2,1)}) %all-gather.2.cloned.1.call-update) | async-done | bytes 26214416 | tf_op jit(solution)/shard_map/all_gather | solution.py:242
  186.7 5.7 fusion.22.refs_0_.refs_1_.refs_2_
  192.5 15.1 %shard_map.152.r2_ref = bf16[4,408,256]{2,1,0:T(8,128)(2,1)S(1)} custom-call(f32[4,536,768]{2,1,0:T(8,128)S(1)} %fusion.22.refs_0_.refs_1_.refs_2_, f32[4,536,768]{2,1,0:T(8,128)S(1)} %fusion.22.refs_0_.refs_1_.refs_2_, f32[4,536,768]{2,1,0:T(8,128)S(1)} %fusion.22.refs_0_.refs_1_.refs_2_, f32[536,128]{1,0:T(8,128)S(1)} %get-tuple-element.77.refs_3_, ...), custom_call_target="tpu_custom_call" | custom-call | tf_op jit(solution)/shard_map/pallas_call | solution.py:155
  207.6 3.1 fusion.83
  212.3 8.4 %fusion.4 = f32[4,408,1312]{2,1,0:T(8,128)S(1)} fusion(bf16[4,1024,3200]{2,1,0:T(8,128)(2,1)} %bitcast.82, bf16[408,1024]{1,0:T(8,128)(2,1)S(1)} %multiply_convert_fusion.1.l1_ref), kind=kOutput, calls=%fused_computation.6 | convolution fusion | flops 4385144832 | bytes 20934656 | tf_op jit(solution)/shard_map/nd,tdk->tnk/dot_general | solution.py:222
  220.8 15.5 %bitcast_multiply_fusion.1 = (f32[4,408,656]{2,1,0:T(8,128)}, f32[4,408,656]{2,1,0:T(8,128)S(1)}, f32[4,656,408]{1,2,0:T(8,128)S(1)}) fusion(f32[4,408,1312]{2,1,0:T(8,128)S(1)} %fusion.4, bf16[408,1024]{1,0:T(8,128)(2,1)S(1)} %copy-done.10, bf16[4,1024,3200]{2,1,0:T(8,128)(2,1)} %bitcast.83), kind=kOutput, calls=%fused_computation.17 | convolution fusion | flops 2262160896 | bytes 24256512 | tf_op jit(solution)/shard_map/nd,tdf->tnf/dot_general | solution.py:222
  236.3 4.5 multiply_add_fusion
  240.8 6.0 add_convert_fusion.r1_ref
  246.8 1.1 copy-done.13
  248.0 16.7 %shard_map.153 = bf16[4096,1968]{1,0:T(8,128)(2,1)} custom-call(bf16[408,1024]{1,0:T(8,128)(2,1)S(1)} %copy-done.13, bf16[4,408,1312]{2,1,0:T(8,128)(2,1)S(1)} %add_convert_fusion.r1_ref, bf16[408,1024]{1,0:T(8,128)(2,1)S(1)} %copy-done.10, bf16[4,408,656]{2,1,0:T(8,128)(2,1)S(1)} %get-tuple-element.61.r2_ref), custom_call_target="tpu_custom_call" | custom-call | tf_op jit(solution)/shard_map/pallas_call | solution.py:193
  264.6 2.1 copy-done.4
  267.9 2.0 pad_maximum_fusion.l1_ref
  269.9 12.4 %fusion.40 = (f32[1024]{0:T(1024)S(1)}, f32[408]{0:T(512)S(1)}, f32[408,1024,1]{1,0,2:T(8,128)}) fusion(f32[408,1024]{1,0:T(8,128)S(1)} %copy-done.25, f32[408]{0:T(512)S(1)} %fusion.75, f32[408]{0:T(512)S(1)} %broadcast_multiply_fusion, f32[1024]{0:T(1024)S(1)} %copy-done.31, bf16[4,408,1312]{2,1,0:T(8,128)(2,1)} %copy-done.4, ...), kind=kOutput, calls=%fused_computation.61 | convolution fusion | flops 4388067840 | bytes 19485472 | tf_op jit(solution)/shard_map/tnk,tdk->nd/dot_general | solution.py:222
  282.3 2.2 fusion.78
  284.9 3.4 fusion.55.refs_6_
  288.3 31.5 %shard_map.154.r1_ref = bf16[4,536,768]{2,1,0:T(8,128)(2,1)S(1)} custom-call(f32[4,536,768]{2,1,0:T(8,128)S(1)} %bitcast.64, f32[4,536,768]{2,1,0:T(8,128)S(1)} %bitcast.64, f32[4,536,768]{2,1,0:T(8,128)S(1)} %bitcast.64, f32[536,128]{1,0:T(8,128)S(1)} %copy-done.17, f32[536,128]{1,0:T(8,128)S(1)} %copy-done.19, f32[408,536]{1,0:T(8,128)S(1)} %copy-done.9, ...), custom_call_target="tpu_custom_call" | custom-call | tf_op jit(solution)/shard_map/pallas_call | solution.py:170
  319.8 10.6 %shard_map.155 = bf16[4096,1024]{1,0:T(8,128)(2,1)S(1)} custom-call(bf16[536,1024]{1,0:T(8,128)(2,1)S(1)} %copy-done.11, bf16[4,536,768]{2,1,0:T(8,128)(2,1)S(1)} %shard_map.154.r1_ref, bf16[408,1024]{1,0:T(8,128)(2,1)S(1)} %fusion.59.l2_ref, bf16[4,408,256]{2,1,0:T(8,128)(2,1)S(1)} %copy-done.15), custom_call_target="tpu_custom_call" | custom-call | tf_op jit(solution)/shard_map/pallas_call | solution.py:193
  330.5 3.3 copy-done.3
  333.8 1.8 copy-done.5
  335.6 112.4 %reduce-scatter.3.cloned.1.call-done = bf16[128,1968]{1,0:T(8,128)(2,1)} async-done(((bf16[4096,1968]{1,0:T(8,128)(2,1)}), bf16[128,1968]{1,0:T(8,128)(2,1)}) %reduce-scatter.3.cloned.1.call-update) | async-done | bytes 503824 | tf_op jit(solution)/shard_map/reduce_scatter | solution.py:292
  448.0 6.9 %fusion.84 = (bf16[536,1024]{1,0:T(8,128)(2,1)S(1)}, f32[536,1024]{1,0:T(8,128)S(1)}) fusion(bf16[4,536,768]{2,1,0:T(8,128)(2,1)} %copy-done.5, bf16[4,1024,3200]{2,1,0:T(8,128)(2,1)} %bitcast.86), kind=kOutput, calls=%fused_computation.129 | convolution fusion | flops 3372769280 | bytes 12877824 | tf_op jit(solution)/shard_map/tnk,tdk->nd/dot_general | solution.py:222
  455.0 1.3 collective-permute-start.2
  456.3 1.3 collective-permute-start.3
  457.6 2.3 collective-permute-done.2
  459.9 8.0 %collective-permute-done.3 = bf16[64,1024]{1,0:T(8,128)(2,1)S(1)} collective-permute-done((bf16[64,1024]{1,0:T(8,128)(2,1)S(1)}, bf16[64,1024]{1,0:T(8,128)(2,1)S(1)}, u32[]{:S(2)}, u32[]{:S(2)}) %collective-permute-start.3) | collective-permute-done | bytes 131104 | tf_op jit(solution)/shard_map/ppermute | solution.py:313
  469.6 6.5 %fusion.41 = bf16[408,1024]{1,0:T(8,128)(2,1)} fusion(f32[408,1024]{1,0:T(8,128)S(1)} %copy-done.26, bf16[4,408,656]{2,1,0:T(8,128)(2,1)S(1)} %copy-done.7, bf16[4,1024,3200]{2,1,0:T(8,128)(2,1)} %bitcast.87), kind=kOutput, calls=%fused_computation.63 | convolution fusion | flops 2193408000 | bytes 10939392 | tf_op jit(solution)/shard_map/tnf,tdf->nd/dot_general | solution.py:222
  476.2 3.6 collective-permute-done.5
  479.9 1.1 collective-permute-start.6
  481.6 2.0 collective-permute-done.6
  484.6 2.6 collective-permute-done.7
  487.3 1.8 collective-permute-start.8
  489.1 1.3 add_convert_fusion.1
  490.4 1.4 collective-permute-done.8
  492.5 1.1 convert_element_type.74
  494.7 1.2 slice_bitcast_fusion
  496.8 105.2 %reduce-scatter.5.cloned.1.call-done = bf16[128,1024]{1,0:T(8,128)(2,1)} async-done(((bf16[4096,1024]{1,0:T(8,128)(2,1)}), bf16[128,1024]{1,0:T(8,128)(2,1)}) %reduce-scatter.5.cloned.1.call-update) | async-done | bytes 262160 | tf_op jit(solution)/shard_map/reduce_scatter | solution.py:306
  (125 shorter events, 17.8 us)
Async XLA Ops:
  7.2 11.7 %copy-start = (bf16[1024,2,656]{0,2,1:T(8,128)(2,1)S(1)}, bf16[1024,2,656]{0,2,1:T(8,128)(2,1)}, u32[]{:S(2)}) copy-start(bf16[1024,2,656]{0,2,1:T(8,128)(2,1)} %param.15) | copy-start | bytes 8060932
  7.2 15.8 %copy-start.20 = (bf16[408,1024]{1,0:T(8,128)(2,1)S(1)}, bf16[408,1024]{1,0:T(8,128)(2,1)}, u32[]{:S(2)}) copy-start(bf16[408,1024]{1,0:T(8,128)(2,1)} %param.9) | copy-start | bytes 2506756
  7.2 16.4 %copy-start.30 = (f32[1024]{0:T(1024)S(1)}, f32[1024]{0:T(1024)}, u32[]{:S(2)}) copy-start(f32[1024]{0:T(1024)} %param.11) | copy-start | bytes 12292
  7.2 179.5 %all-gather.2.cloned.1.call-start = ((), (), s32[]{:S(2)}) async-start(), calls=%async_computation.2 | async-start | bytes 27033600 | tf_op jit(solution)/shard_map/all_gather | solution.py:242
  12.1 18.9 %copy-start.32 = (s32[25]{0:T(128)S(1)}, s32[25]{0:T(128)}, u32[]{:S(2)}) copy-start(s32[25]{0:T(128)} %param.10) | copy-start | bytes 304
  22.9 425.0 %reduce-scatter.3.cloned.1.call-start = ((), (), s32[]{:S(2)}) async-start(), calls=%async_computation.3 | async-start | bytes 17301504 | tf_op jit(solution)/shard_map/reduce_scatter | solution.py:292
  23.9 168.6 %copy-start.27 = (bf16[408,1024]{1,0:T(8,128)(2,1)}, bf16[408,1024]{1,0:T(8,128)(2,1)S(1)}, u32[]{:S(2)}) copy-start(bf16[408,1024]{1,0:T(8,128)(2,1)S(1)} %fusion.35) | copy-start | bytes 2506756
  24.7 8.6 %collective-permute-start = (bf16[64,1024]{1,0:T(8,128)(2,1)}, bf16[64,1024]{1,0:T(8,128)(2,1)S(1)}, u32[]{:S(2)}, u32[]{:S(2)}) collective-permute-start(bf16[64,1024]{1,0:T(8,128)(2,1)} %get-tuple-element.64), channel_id=1, source_target_pairs={{0,1},{1,2},{2,3},{3,4},{4,5},{5,6},{6,7},{7,8},{8,9},{9,10},{10,1... | collective-permute-start | bytes 393224 | tf_op jit(solution)/shard_map/ppermute | solution.py:258
  29.6 12.0 %collective-permute-start.1 = (bf16[64,1024]{1,0:T(8,128)(2,1)}, bf16[64,1024]{1,0:T(8,128)(2,1)}, u32[]{:S(2)}, u32[]{:S(2)}) collective-permute-start(bf16[64,1024]{1,0:T(8,128)(2,1)} %get-tuple-element.65), channel_id=1, source_target_pairs={{1,0},{2,1},{3,2},{4,3},{5,4},{6,5},{7,6},{8,7},{9,8},{10,9},{11,1... | collective-permute-start | bytes 393224 | tf_op jit(solution)/shard_map/ppermute | solution.py:260
  31.7 160.8 %copy-start.8 = (f32[408,536]{1,0:T(8,128)}, f32[408,536]{1,0:T(8,128)S(1)}, u32[]{:S(2)}) copy-start(f32[408,536]{1,0:T(8,128)S(1)} %fusion.61.refs_5_) | copy-start | bytes 2624260
  33.2 159.3 %copy-start.16 = (f32[536,128]{1,0:T(8,128)}, f32[536,128]{1,0:T(8,128)S(1)}, u32[]{:S(2)}) copy-start(f32[536,128]{1,0:T(8,128)S(1)} %get-tuple-element.77.refs_3_) | copy-start | bytes 823300
  33.3 159.3 %copy-start.18 = (f32[536,128]{1,0:T(8,128)}, f32[536,128]{1,0:T(8,128)S(1)}, u32[]{:S(2)}) copy-start(f32[536,128]{1,0:T(8,128)S(1)} %get-tuple-element.78.refs_4_) | copy-start | bytes 823300
  192.5 15.1 %copy-start.2 = (f32[4,536,768]{2,1,0:T(8,128)}, f32[4,536,768]{2,1,0:T(8,128)S(1)}, u32[]{:S(2)}) copy-start(f32[4,536,768]{2,1,0:T(8,128)S(1)} %fusion.22.refs_0_.refs_1_.refs_2_) | copy-start | bytes 19759108
  207.6 3.1 copy-start.14
  207.6 4.4 copy-start.31
  210.7 1.3 copy-start.24
  212.3 8.5 %copy-start.12 = (bf16[408,1024]{1,0:T(8,128)(2,1)}, bf16[408,1024]{1,0:T(8,128)(2,1)S(1)}, u32[]{:S(2)}) copy-start(bf16[408,1024]{1,0:T(8,128)(2,1)S(1)} %multiply_convert_fusion.1.l1_ref) | copy-start | bytes 2506756
  212.3 8.5 %copy-start.10 = (bf16[408,1024]{1,0:T(8,128)(2,1)S(1)}, bf16[408,1024]{1,0:T(8,128)(2,1)}, u32[]{:S(2)}) copy-start(bf16[408,1024]{1,0:T(8,128)(2,1)} %l2_ref.1) | copy-start | bytes 2506756
  240.8 6.0 copy-start.6
  246.8 1.2 copy-start.13
  264.6 2.1 copy-start.4
  266.8 1.1 copy-start.28
  266.8 3.1 copy-start.25
  266.8 335.1 %reduce-scatter.5.cloned.1.call-start = ((), (), s32[]{:S(2)}) async-start(), calls=%async_computation.4 | async-start | bytes 8650752 | tf_op jit(solution)/shard_map/reduce_scatter | solution.py:306
  282.3 5.9 slice-start
  284.6 3.7 copy-start.22
  284.6 3.7 slice-start.1
  284.6 3.7 copy-start.9
  284.6 3.7 copy-start.17
  284.6 3.7 copy-start.19
  288.3 31.5 %copy-start.11 = (bf16[536,1024]{1,0:T(8,128)(2,1)S(1)}, bf16[536,1024]{1,0:T(8,128)(2,1)}, u32[]{:S(2)}) copy-start(bf16[536,1024]{1,0:T(8,128)(2,1)} %pad_maximum_fusion.l1_ref) | copy-start | bytes 3293188
  288.3 31.5 %copy-start.15 = (bf16[4,408,256]{2,1,0:T(8,128)(2,1)S(1)}, bf16[4,408,256]{2,1,0:T(8,128)(2,1)}, u32[]{:S(2)}) copy-start(bf16[4,408,256]{2,1,0:T(8,128)(2,1)} %copy-done.14) | copy-start | bytes 2506756
  330.5 3.3 copy-start.3
  333.8 1.8 copy-start.5
  448.0 19.9 %copy-start.21 = (bf16[408,1024]{1,0:T(8,128)(2,1)S(1)}, bf16[408,1024]{1,0:T(8,128)(2,1)}, u32[]{:S(2)}) copy-start(bf16[408,1024]{1,0:T(8,128)(2,1)} %param.9) | copy-start | bytes 2506756
  448.0 21.6 %copy-start.7 = (bf16[4,408,656]{2,1,0:T(8,128)(2,1)S(1)}, bf16[4,408,656]{2,1,0:T(8,128)(2,1)}, u32[]{:S(2)}) copy-start(bf16[4,408,656]{2,1,0:T(8,128)(2,1)} %copy-done.6) | copy-start | bytes 6423556
  448.0 21.5 %copy-start.26 = (f32[408,1024]{1,0:T(8,128)S(1)}, f32[408,1024]{1,0:T(8,128)}, u32[]{:S(2)}) copy-start(f32[408,1024]{1,0:T(8,128)} %copy-done.24) | copy-start | bytes 5013508
  455.0 4.9 collective-permute-start.2
  456.3 11.6 %collective-permute-start.3 = (bf16[64,1024]{1,0:T(8,128)(2,1)S(1)}, bf16[64,1024]{1,0:T(8,128)(2,1)S(1)}, u32[]{:S(2)}, u32[]{:S(2)}) collective-permute-start(bf16[64,1024]{1,0:T(8,128)(2,1)S(1)} %get-tuple-element.63), channel_id=1, source_target_pairs={{1,0},{2,1},{3,2},{4,3},{5,4},{6,5},{7,6},{8,7},{9,8},{10,9},{11,1... | collective-permute-start | bytes 393224 | tf_op jit(solution)/shard_map/ppermute | solution.py:313
  468.5 7.6 %collective-permute-start.4 = (f32[2,1024]{1,0:T(2,128)S(1)}, f32[2,1024]{1,0:T(2,128)S(1)}, u32[]{:S(2)}, u32[]{:S(2)}) collective-permute-start(f32[2,1024]{1,0:T(2,128)S(1)} %pad_maximum_fusion.3), channel_id=1, source_target_pairs={{0,4},{4,0},{8,12},{12,8},{16,20},{20,16},{24,28},{28,24},{1,5},{5... | collective-permute-start | bytes 24584 | tf_op jit(solution)/shard_map/ppermute | solution.py:216
  476.1 13.0 %copy-start.23 = (f32[408,1024]{1,0:T(8,128)S(1)}, f32[408,1024]{1,0:T(8,128)}, u32[]{:S(2)}) copy-start(f32[408,1024]{1,0:T(8,128)} %copy-done.22) | copy-start | bytes 5013508
  476.1 3.7 collective-permute-start.5
  479.9 12.6 %copy-start.29 = (bf16[128,1968]{1,0:T(8,128)(2,1)S(1)}, bf16[128,1968]{1,0:T(8,128)(2,1)}, u32[]{:S(2)}) copy-start(bf16[128,1968]{1,0:T(8,128)(2,1)} %reduce-scatter.3.cloned.1.call-done) | copy-start | bytes 1511428
  479.9 3.8 collective-permute-start.6
  483.6 3.7 collective-permute-start.7
  487.3 4.6 collective-permute-start.8
  491.8 113.9 %copy-start.1 = (bf16[1024,2,656]{0,2,1:T(8,128)(2,1)S(1)}, bf16[1024,2,656]{0,2,1:T(8,128)(2,1)}, u32[]{:S(2)}) copy-start(bf16[1024,2,656]{0,2,1:T(8,128)(2,1)} %param.15) | copy-start | bytes 8060932
Sparse Core Ops, SparseCore 0:
  23.0 163.6 all-gather.1
  266.9 180.9 reduce-scatter.2
  450.3 151.6 reduce-scatter.4

commit v3 on v2

--- a/solution.py
+++ b/solution.py
@@ -218,6 +218,28 @@
     return value
 
 
+def halving_sum(terms, deep, reverse):
+    dp, tp = lax.axis_size("dp"), lax.axis_size("tensor")
+    dp_bits, tp_bits = dp.bit_length() - 1, tp.bit_length() - 1
+    order = list(range(1, dp_bits))
+    steps = [("dp", bit) for bit in [0] + (order[::-1] if reverse else order)]
+    steps += [("tensor", bit) for bit in range(tp_bits)]
+    dims = [("tensor", bit) for bit in reversed(range(tp_bits))]
+    dims += [("dp", bit) for bit in reversed(range(dp_bits))]
+    value = terms.reshape([2] * len(dims) + [deep, terms.shape[1]])
+    for step in steps:
+        name, bit = step
+        place = dims.index(step)
+        dims.pop(place)
+        mine = (lax.axis_index(name) >> bit) & 1
+        keep = lax.dynamic_index_in_dim(value, mine, place, keepdims=False)
+        send = lax.dynamic_index_in_dim(value, 1 - mine, place, keepdims=False)
+        pairs = [(i, i ^ (1 << bit)) for i in range(lax.axis_size(name))]
+        got = lax.ppermute(send, name, pairs)
+        value = (keep.astype(F32) + got.astype(F32)).astype(BF)
+    return value
+
+
 def ein(spec, a, b):
     return jnp.einsum(spec, a, b, preferred_element_type=F32)
 
@@ -302,12 +324,13 @@
     grad_mixed = ein("nd,tdc->tnc", grad_res_low, all_out).astype(BF)
     grad_qkv_low = attend_bwd(rows, projected, cosine, sine, bias, grad_mixed)
     attn_terms = pair_products(normed_ext, grad_qkv_low, grad_res_low, mixed)
-    attn_terms, ffn_sum = lax.optimization_barrier((attn_terms, ffn_sum))
-    attn_sum = lax.psum_scatter(
-        attn_terms,
-        PIECES,
-        scatter_dimension=0,
-        tiled=True,
+    middle = attn_terms.shape[1] // 2
+    attn_sum = jnp.concatenate(
+        [
+            halving_sum(attn_terms[:, :middle], deep, False),
+            halving_sum(attn_terms[:, middle:], deep, True),
+        ],
+        axis=1,
     )
     grad_normed_ext = ein("tnk,tdk->nd", grad_qkv_low, all_qkv)
     from_after = lax.ppermute(grad_normed_ext[:HALF].astype(BF), ROWS, backward)

time: 613 us -> 499 us (0.81)
  waiting for transfers between devices: 391 us -> 241 us
  starting transfers between devices: 14 us -> 25.6 us
  local copies, waits for them, and re-layouts: 31.8 us -> 42 us
  other arithmetic: 25.2 us -> 33.3 us
    reduce_scatter x1, waiting for transfers between devices: 112 us -> 1.96 us  [body(): lax.psum_scatter(ffn_terms, PIECES, scatter_dimension=0, tiled=True)]
    reduce_scatter x1 -> x0, waiting for transfers between devices: 105 us -> none  [body(): lax.psum_scatter(attn_terms, PIECES, scatter_dimension=0, tiled=True)]
    ppermute x0 -> x10, waiting for transfers between devices: none -> 77.2 us  [halving_sum(): got = lax.ppermute(send, name, pairs)]
    dynamic_slice x0 -> x4, local copies, waits for them, and re-layouts: none -> 10.7 us  [the longest x2 6.72 us: halving_sum(): send = lax.dynamic_index_in_dim(value, 1 - mine, place, keepdims=False)]
    ppermute x0 -> x10, starting transfers between devices: none -> 10.4 us  [halving_sum(): got = lax.ppermute(send, name, pairs)]
    ppermute x1, waiting for transfers between devices: 7.97 us -> 0.01 us  [body(): from_after = lax.ppermute(grad_normed_ext[:HALF].astype(BF), ROWS, backward)]
    convert_element_type x0 -> x10, other arithmetic: none -> 6.16 us  [halving_sum(): value = (keep.astype(F32) + got.astype(F32)).astype(BF)]
    unnamed x76 -> x87, local copies, waits for them, and re-layouts: 18.2 us -> 16.9 us
  transfers between devices with their start and end apart: 12 -> 21, of which waited for: 10 -> 11; matrix products, arithmetic and copies ran while one was open for 7% -> 15% of each run, Pallas kernels for 7% -> 8%
where the time goes in v3:
time: 499 us; the launch traced here: 495 us
  waiting for transfers between devices  241 us (48%)
  Pallas kernels  73.7 us (15%)
  matrix products  64.3 us (13%)
  local copies, waits for them, and re-layouts  42 us (8%)
  other arithmetic  33.3 us (7%)
  starting transfers between devices  25.6 us (5%)
  between operations  15.1 us (3%)
    all_gather x1, waiting for transfers between devices, body(): gathered = lax.all_gather(piece, PIECES, axis=0, tiled=True)  145 us
    ppermute x10, waiting for transfers between devices, halving_sum(): got = lax.ppermute(send, name, pairs)  77.2 us
    dot_general x8, matrix products, ein(): return jnp.einsum(spec, a, b, preferred_element_type=F32)  64.3 us
    pallas_call x1, Pallas kernels, attend_bwd(): pl.pallas_call(lambda *refs: bwd_kernel(rows, *refs), grid=(tp * per, 3),...  31.2 us
    pallas_call x2, Pallas kernels, pair_products(): pl.pallas_call(pair_kernel, grid=(tp, count), in_specs=[pl.BlockSpec((n1,...  27.4 us
    unnamed x87, local copies, waits for them, and re-layouts  16.9 us
    pallas_call x1, Pallas kernels, attend_fwd(): pl.pallas_call(lambda *refs: fwd_kernel(rows, *refs), grid=(tp * per,), i...  15.1 us
    ppermute x10, starting transfers between devices, halving_sum(): got = lax.ppermute(send, name, pairs)  10.4 us
  transfers between devices with their start and end apart: 21, of which 11 were waited for; matrix products, arithmetic and copies ran while one was open for 15% of the time, Pallas kernels for 8%

profile of v3, /device:TPU:0, one launch (start us, length us, event | category | flops | bytes accessed | tf_op | source)
XLA Modules:
  0.0 495.0 jit_solution(13686438302725553984)
XLA Ops:
  7.2 1.7 copy-done
  17.1 4.9 collective-permute-start
  25.7 8.3 %collective-permute-done.1 = bf16[64,1024]{1,0:T(8,128)(2,1)} collective-permute-done((bf16[64,1024]{1,0:T(8,128)(2,1)}, bf16[64,1024]{1,0:T(8,128)(2,1)}, u32[]{:S(2)}, u32[]{:S(2)}) %collective-permute-start.1) | collective-permute-done | bytes 131104 | tf_op jit(solution)/shard_map/ppermute | solution.py:282
  34.0 145.1 %all-gather.2.cloned.1.call-done = bf16[4096,3200]{1,0:T(8,128)(2,1)} async-done(((bf16[128,3200]{1,0:T(8,128)(2,1)}), bf16[4096,3200]{1,0:T(8,128)(2,1)}) %all-gather.2.cloned.1.call-update) | async-done | bytes 26214416 | tf_op jit(solution)/shard_map/all_gather | solution.py:264
  179.1 5.9 %fusion.24.refs_0_.refs_1_.refs_2_ = f32[4,536,768]{2,1,0:T(8,128)S(1)} fusion(bf16[4,1024,3200]{2,1,0:T(8,128)(2,1)} %bitcast.134, bf16[64,1024]{1,0:T(8,128)(2,1)} %collective-permute-done.1, bf16[408,1024]{1,0:T(8,128)(2,1)S(1)} %fusion.39, bf16[64,1024]{1,0:T(8,128)(2,1)S(1)} %collective-permute-done), kind=kOutput, calls=%fused_computation.39 | convolution fusion | flops 3375513600 | bytes 13975552 | tf_op jit(solution)/shard_map/nd,tdk->tnk/dot_general | solution.py:244
  185.1 15.1 %shard_map.152.r2_ref = bf16[4,408,256]{2,1,0:T(8,128)(2,1)S(1)} custom-call(f32[4,536,768]{2,1,0:T(8,128)S(1)} %fusion.24.refs_0_.refs_1_.refs_2_, f32[4,536,768]{2,1,0:T(8,128)S(1)} %fusion.24.refs_0_.refs_1_.refs_2_, f32[4,536,768]{2,1,0:T(8,128)S(1)} %fusion.24.refs_0_.refs_1_.refs_2_, f32[536,128]{1,0:T(8,128)S(1)} %get-tuple-element.79.refs_3_, ...), custom_call_target="tpu_custom_call" | custom-call | tf_op jit(solution)/shard_map/pallas_call | solution.py:155
  200.2 3.1 fusion.94
  204.8 8.4 %fusion.4 = f32[4,408,1312]{2,1,0:T(8,128)S(1)} fusion(bf16[4,1024,3200]{2,1,0:T(8,128)(2,1)} %bitcast.136, bf16[408,1024]{1,0:T(8,128)(2,1)S(1)} %multiply_convert_fusion.1.l1_ref), kind=kOutput, calls=%fused_computation.6 | convolution fusion | flops 4385144832 | bytes 20934656 | tf_op jit(solution)/shard_map/nd,tdk->tnk/dot_general | solution.py:244
  213.2 15.6 %bitcast_multiply_fusion.1 = (f32[4,408,656]{2,1,0:T(8,128)}, f32[4,408,656]{2,1,0:T(8,128)S(1)}, f32[4,656,408]{1,2,0:T(8,128)S(1)}) fusion(f32[4,408,1312]{2,1,0:T(8,128)S(1)} %fusion.4, bf16[408,1024]{1,0:T(8,128)(2,1)S(1)} %copy-done.9, bf16[4,1024,3200]{2,1,0:T(8,128)(2,1)} %bitcast.137), kind=kOutput, calls=%fused_computation.17 | convolution fusion | flops 2262160896 | bytes 24256512 | tf_op jit(solution)/shard_map/nd,tdf->tnf/dot_general | solution.py:244
  228.8 5.0 %multiply_add_fusion = (f32[4,408,656]{2,1,0:T(8,128)}, bf16[4,408,656]{2,1,0:T(8,128)(2,1)S(1)}) fusion(f32[4,408,656]{2,1,0:T(8,128)S(1)} %get-tuple-element.55, f32[4,656,408]{1,2,0:T(8,128)S(1)} %get-tuple-element.75, f32[4,408,1312]{2,1,0:T(8,128)S(1)} %fusion.4), kind=kLoop, calls=%fused_computation.18 | loop fusion | flops 18200064 | bytes 23553024 | tf_op jit(solution)/shard_map/transpose(jvp())/add_any | solution.py:303
  233.8 6.0 %add_convert_fusion.r1_ref = bf16[4,408,1312]{2,1,0:T(8,128)(2,1)S(1)} fusion(f32[4,408,656]{2,1,0:T(8,128)} %get-tuple-element.56, f32[4,408,656]{2,1,0:T(8,128)} %get-tuple-element.54), kind=kLoop, calls=%fused_computation.4 | loop fusion | flops 4282368 | bytes 12847104 | tf_op jit(solution)/shard_map/convert_element_type | solution.py:311
  241.0 16.7 %shard_map.153 = bf16[4096,1968]{1,0:T(8,128)(2,1)} custom-call(bf16[408,1024]{1,0:T(8,128)(2,1)S(1)} %copy-done.12, bf16[4,408,1312]{2,1,0:T(8,128)(2,1)S(1)} %add_convert_fusion.r1_ref, bf16[408,1024]{1,0:T(8,128)(2,1)S(1)} %copy-done.9, bf16[4,408,656]{2,1,0:T(8,128)(2,1)S(1)} %get-tuple-element.57.r2_ref), custom_call_target="tpu_custom_call" | custom-call | tf_op jit(solution)/shard_map/pallas_call | solution.py:193
  257.7 2.0 copy-done.3
  260.9 2.0 pad_maximum_fusion.l1_ref
  262.9 12.4 %fusion.44 = (f32[1024]{0:T(1024)S(1)}, f32[408]{0:T(512)S(1)}, f32[408,1024,1]{1,0,2:T(8,128)}) fusion(f32[408,1024]{1,0:T(8,128)S(1)} %copy-done.23, f32[408]{0:T(512)S(1)} %fusion.85, f32[408]{0:T(512)S(1)} %broadcast_multiply_fusion, f32[1024]{0:T(1024)S(1)} %copy-done.36, bf16[4,408,1312]{2,1,0:T(8,128)(2,1)} %copy-done.3, ...), kind=kOutput, calls=%fused_computation.69 | convolution fusion | flops 4388067840 | bytes 19485472 | tf_op jit(solution)/shard_map/tnk,tdk->nd/dot_general | solution.py:244
  275.3 2.2 fusion.88
  277.9 3.4 fusion.59.refs_6_
  281.3 31.2 %shard_map.154.r1_ref = bf16[4,536,768]{2,1,0:T(8,128)(2,1)S(1)} custom-call(f32[4,536,768]{2,1,0:T(8,128)S(1)} %bitcast.114, f32[4,536,768]{2,1,0:T(8,128)S(1)} %bitcast.114, f32[4,536,768]{2,1,0:T(8,128)S(1)} %bitcast.114, f32[536,128]{1,0:T(8,128)S(1)} %copy-done.16, f32[536,128]{1,0:T(8,128)S(1)} %copy-done.18, f32[408,536]{1,0:T(8,128)S(1)} %copy-done.8, ...), custom_call_target="tpu_custom_call" | custom-call | tf_op jit(solution)/shard_map/pallas_call | solution.py:170
  312.6 10.6 %shard_map.155 = bf16[4096,1024]{1,0:T(8,128)(2,1)S(1)} custom-call(bf16[536,1024]{1,0:T(8,128)(2,1)S(1)} %copy-done.10, bf16[4,536,768]{2,1,0:T(8,128)(2,1)S(1)} %shard_map.154.r1_ref, bf16[408,1024]{1,0:T(8,128)(2,1)S(1)} %fusion.63.l2_ref, bf16[4,408,256]{2,1,0:T(8,128)(2,1)S(1)} %copy-done.14), custom_call_target="tpu_custom_call" | custom-call | tf_op jit(solution)/shard_map/pallas_call | solution.py:193
  323.2 2.7 fusion.90
  325.9 1.6 constant_dynamic-slice_fusion.3
  327.5 2.4 copy.78
  330.2 9.0 %fusion.95 = (bf16[536,1024]{1,0:T(8,128)(2,1)S(1)}, f32[536,1024]{1,0:T(8,128)}) fusion(bf16[4,536,768]{2,1,0:T(8,128)(2,1)} %copy-done.4, bf16[4,1024,3200]{2,1,0:T(8,128)(2,1)} %bitcast.140), kind=kOutput, calls=%fused_computation.163 | convolution fusion | flops 3372769280 | bytes 12877824 | tf_op jit(solution)/shard_map/tnk,tdk->nd/dot_general | solution.py:244
  339.9 1.5 collective-permute-start.2
  342.7 2.3 constant_dynamic-slice_fusion.1
  345.0 4.3 copy.80
  349.4 4.8 collective-permute-start.14
  354.1 2.4 fusion.40
  356.8 6.6 %fusion.45 = bf16[408,1024]{1,0:T(8,128)(2,1)} fusion(f32[408,1024]{1,0:T(8,128)S(1)} %copy-done.24, bf16[4,408,656]{2,1,0:T(8,128)(2,1)S(1)} %copy-done.6, bf16[4,1024,3200]{2,1,0:T(8,128)(2,1)} %bitcast.141), kind=kOutput, calls=%fused_computation.71 | convolution fusion | flops 2193408000 | bytes 10939392 | tf_op jit(solution)/shard_map/tnf,tdf->nd/dot_general | solution.py:244
  363.3 4.3 copy.91
  367.7 2.4 copy.92
  370.0 2.4 collective-permute-start.5
  372.5 1.6 collective-permute-done.5
  374.1 3.4 collective-permute-start.6
  377.5 2.8 fusion.23
  380.7 2.3 fusion.22
  384.1 1.6 fusion.87
  385.8 3.6 collective-permute-done.7
  390.7 3.3 collective-permute-done.8
  394.1 34.3 %collective-permute-done.10 = bf16[2,2,2,128,512]{3,4,0,1,2:T(8,128)(2,1)S(1)} collective-permute-done((bf16[2,2,2,128,512]{3,4,0,1,2:T(8,128)(2,1)S(1)}, bf16[2,2,2,128,512]{3,4,0,1,2:T(8,128)(2,1)S(1)}, u32[]{:S(2)}, u32[]{:S(2)}) %collective-permute-start.10) | collective-permute-done | bytes 1048608 | tf_op jit(solution)/shard_map/ppermute | solution.py:238
  431.3 16.6 %collective-permute-done.11 = bf16[2,2,128,512]{2,3,0,1:T(8,128)(2,1)S(1)} collective-permute-done((bf16[2,2,128,512]{2,3,0,1:T(8,128)(2,1)S(1)}, bf16[2,2,128,512]{2,3,0,1:T(8,128)(2,1)S(1)}, u32[]{:S(2)}, u32[]{:S(2)}) %collective-permute-start.11) | collective-permute-done | bytes 524320 | tf_op jit(solution)/shard_map/ppermute | solution.py:238
  448.1 7.5 %collective-permute-done.16 = bf16[2,2,128,512]{2,3,0,1:T(8,128)(2,1)S(1)} collective-permute-done((bf16[2,2,128,512]{2,3,0,1:T(8,128)(2,1)S(1)}, bf16[2,2,128,512]{2,3,0,1:T(8,128)(2,1)S(1)}, u32[]{:S(2)}, u32[]{:S(2)}) %collective-permute-start.16) | collective-permute-done | bytes 524320 | tf_op jit(solution)/shard_map/ppermute | solution.py:238
  456.6 1.6 collective-permute-start.13
  458.2 10.5 %collective-permute-done.17 = bf16[2,128,512]{1,2,0:T(8,128)(2,1)S(1)} collective-permute-done((bf16[2,128,512]{1,2,0:T(8,128)(2,1)S(1)}, bf16[2,128,512]{1,2,0:T(8,128)(2,1)S(1)}, u32[]{:S(2)}, u32[]{:S(2)}) %collective-permute-start.17) | collective-permute-done | bytes 262176 | tf_op jit(solution)/shard_map/ppermute | solution.py:238
  468.9 8.3 %collective-permute-done.18 = bf16[128,512]{0,1:T(8,128)(2,1)S(1)} collective-permute-done((bf16[128,512]{0,1:T(8,128)(2,1)S(1)}, bf16[128,512]{0,1:T(8,128)(2,1)S(1)}, u32[]{:S(2)}, u32[]{:S(2)}) %collective-permute-start.18) | collective-permute-done | bytes 131104 | tf_op jit(solution)/shard_map/ppermute | solution.py:238
  478.9 2.0 reduce-scatter.2.cloned.1.call-done
  483.0 1.9 copy.83
  485.8 2.2 copy.81
  (175 shorter events, 30.2 us)
Async XLA Ops:
  7.2 172.0 %all-gather.2.cloned.1.call-start = ((), (), s32[]{:S(2)}) async-start(), calls=%async_computation.1 | async-start | bytes 27033600 | tf_op jit(solution)/shard_map/all_gather | solution.py:264
  9.7 5.6 %copy-start.19 = (bf16[408,1024]{1,0:T(8,128)(2,1)S(1)}, bf16[408,1024]{1,0:T(8,128)(2,1)}, u32[]{:S(2)}) copy-start(bf16[408,1024]{1,0:T(8,128)(2,1)} %param.9) | copy-start | bytes 2506756
  12.1 3.8 copy-start.33
  15.3 8.0 %copy-start.37 = (s32[25]{0:T(128)S(1)}, s32[25]{0:T(128)}, u32[]{:S(2)}) copy-start(s32[25]{0:T(128)} %param.10) | copy-start | bytes 304
  15.3 465.5 %reduce-scatter.2.cloned.1.call-start = ((), (), s32[]{:S(2)}) async-start(), calls=%async_computation.2 | async-start | bytes 17301504 | tf_op jit(solution)/shard_map/reduce_scatter | solution.py:314
  15.9 7.8 %copy-start.34 = (f32[408]{0:T(512)}, f32[408]{0:T(512)S(1)}, u32[]{:S(2)}) copy-start(f32[408]{0:T(512)S(1)} %fusion.41) | copy-start | bytes 4900
  16.3 168.8 %copy-start.30 = (bf16[408,1024]{1,0:T(8,128)(2,1)}, bf16[408,1024]{1,0:T(8,128)(2,1)S(1)}, u32[]{:S(2)}) copy-start(bf16[408,1024]{1,0:T(8,128)(2,1)S(1)} %fusion.39) | copy-start | bytes 2506756
  17.1 8.6 %collective-permute-start = (bf16[64,1024]{1,0:T(8,128)(2,1)}, bf16[64,1024]{1,0:T(8,128)(2,1)S(1)}, u32[]{:S(2)}, u32[]{:S(2)}) collective-permute-start(bf16[64,1024]{1,0:T(8,128)(2,1)} %get-tuple-element.66), channel_id=1, source_target_pairs={{0,1},{1,2},{2,3},{3,4},{4,5},{5,6},{6,7},{7,8},{8,9},{9,10},{10,1... | collective-permute-start | bytes 393224 | tf_op jit(solution)/shard_map/ppermute | solution.py:280
  22.0 12.0 %collective-permute-start.1 = (bf16[64,1024]{1,0:T(8,128)(2,1)}, bf16[64,1024]{1,0:T(8,128)(2,1)}, u32[]{:S(2)}, u32[]{:S(2)}) collective-permute-start(bf16[64,1024]{1,0:T(8,128)(2,1)} %get-tuple-element.67), channel_id=1, source_target_pairs={{1,0},{2,1},{3,2},{4,3},{5,4},{6,5},{7,6},{8,7},{9,8},{10,9},{11,1... | collective-permute-start | bytes 393224 | tf_op jit(solution)/shard_map/ppermute | solution.py:282
  24.1 160.9 %copy-start.7 = (f32[408,536]{1,0:T(8,128)}, f32[408,536]{1,0:T(8,128)S(1)}, u32[]{:S(2)}) copy-start(f32[408,536]{1,0:T(8,128)S(1)} %fusion.67.refs_5_) | copy-start | bytes 2624260
  25.7 159.4 %copy-start.15 = (f32[536,128]{1,0:T(8,128)}, f32[536,128]{1,0:T(8,128)S(1)}, u32[]{:S(2)}) copy-start(f32[536,128]{1,0:T(8,128)S(1)} %get-tuple-element.79.refs_3_) | copy-start | bytes 823300
  25.7 159.4 %copy-start.17 = (f32[536,128]{1,0:T(8,128)}, f32[536,128]{1,0:T(8,128)S(1)}, u32[]{:S(2)}) copy-start(f32[536,128]{1,0:T(8,128)S(1)} %get-tuple-element.80.refs_4_) | copy-start | bytes 823300
  185.1 15.1 %copy-start.2 = (f32[4,536,768]{2,1,0:T(8,128)}, f32[4,536,768]{2,1,0:T(8,128)S(1)}, u32[]{:S(2)}) copy-start(f32[4,536,768]{2,1,0:T(8,128)S(1)} %fusion.24.refs_0_.refs_1_.refs_2_) | copy-start | bytes 19759108
  200.2 4.3 copy-start.36
  204.7 8.5 %copy-start.11 = (bf16[408,1024]{1,0:T(8,128)(2,1)}, bf16[408,1024]{1,0:T(8,128)(2,1)S(1)}, u32[]{:S(2)}) copy-start(bf16[408,1024]{1,0:T(8,128)(2,1)S(1)} %multiply_convert_fusion.1.l1_ref) | copy-start | bytes 2506756
  204.8 8.5 %copy-start.9 = (bf16[408,1024]{1,0:T(8,128)(2,1)S(1)}, bf16[408,1024]{1,0:T(8,128)(2,1)}, u32[]{:S(2)}) copy-start(bf16[408,1024]{1,0:T(8,128)(2,1)} %l2_ref.1) | copy-start | bytes 2506756
  233.8 6.0 %copy-start.5 = (bf16[4,408,656]{2,1,0:T(8,128)(2,1)}, bf16[4,408,656]{2,1,0:T(8,128)(2,1)S(1)}, u32[]{:S(2)}) copy-start(bf16[4,408,656]{2,1,0:T(8,128)(2,1)S(1)} %get-tuple-element.57.r2_ref) | copy-start | bytes 6423556
  275.3 5.9 %slice-start = ((s8[6586368]{0:T(1024)(128)(4,1)}), s8[4194304]{0:T(1024)(128)(4,1)S(1)}, s32[]{:S(2)}) async-start(s8[6586368]{0:T(1024)(128)(4,1)} %bitcast.113), calls=%async_computation.3 | async-start | bytes 8388608
  277.6 3.7 slice-start.1
  281.3 31.3 %copy-start.10 = (bf16[536,1024]{1,0:T(8,128)(2,1)S(1)}, bf16[536,1024]{1,0:T(8,128)(2,1)}, u32[]{:S(2)}) copy-start(bf16[536,1024]{1,0:T(8,128)(2,1)} %pad_maximum_fusion.l1_ref) | copy-start | bytes 3293188
  281.3 31.3 %copy-start.14 = (bf16[4,408,256]{2,1,0:T(8,128)(2,1)S(1)}, bf16[4,408,256]{2,1,0:T(8,128)(2,1)}, u32[]{:S(2)}) copy-start(bf16[4,408,256]{2,1,0:T(8,128)(2,1)} %copy-done.13) | copy-start | bytes 2506756
  312.6 10.7 %copy-start.4 = (bf16[4,536,768]{2,1,0:T(8,128)(2,1)}, bf16[4,536,768]{2,1,0:T(8,128)(2,1)S(1)}, u32[]{:S(2)}) copy-start(bf16[4,536,768]{2,1,0:T(8,128)(2,1)S(1)} %shard_map.154.r1_ref) | copy-start | bytes 9879556
  329.9 47.6 %collective-permute-start.9 = (bf16[2,2,2,2,128,512]{4,5,0,1,2,3:T(8,128)(2,1)}, bf16[2,2,2,2,128,512]{4,5,0,1,2,3:T(8,128)(2,1)}, u32[]{:S(2)}, u32[]{:S(2)}) collective-permute-start(bf16[2,2,2,2,128,512]{4,5,0,1,2,3:T(8,128)(2,1)} %bitcast.117), channel_id=1, source_target_pairs={{0,4},{4,0},{8,12},{12,8},{16,20},{20,16},{24,28},{28,24},{1,5},{5... | collective-permute-start | bytes 6291464 | tf_op jit(solution)/shard_map/ppermute | solution.py:238
  330.2 12.5 %copy-start.21 = (bf16[4096,512]{1,0:T(8,128)(2,1)S(1)}, bf16[4096,512]{1,0:T(8,128)(2,1)}, u32[]{:S(2)}) copy-start(bf16[4096,512]{1,0:T(8,128)(2,1)} %get-tuple-element.59) | copy-start | bytes 12582916
  339.9 14.2 %collective-permute-start.2 = (bf16[64,1024]{1,0:T(8,128)(2,1)}, bf16[64,1024]{1,0:T(8,128)(2,1)S(1)}, u32[]{:S(2)}, u32[]{:S(2)}) collective-permute-start(bf16[64,1024]{1,0:T(8,128)(2,1)} %get-tuple-element.64), channel_id=1, source_target_pairs={{0,1},{1,2},{2,3},{3,4},{4,5},{5,6},{6,7},{7,8},{8,9},{9,10},{10,1... | collective-permute-start | bytes 393224 | tf_op jit(solution)/shard_map/ppermute | solution.py:337
  341.4 12.7 %collective-permute-start.3 = (bf16[64,1024]{1,0:T(8,128)(2,1)}, bf16[64,1024]{1,0:T(8,128)(2,1)}, u32[]{:S(2)}, u32[]{:S(2)}) collective-permute-start(bf16[64,1024]{1,0:T(8,128)(2,1)} %get-tuple-element.65), channel_id=1, source_target_pairs={{1,0},{2,1},{3,2},{4,3},{5,4},{6,5},{7,6},{8,7},{9,8},{10,9},{11,1... | collective-permute-start | bytes 393224 | tf_op jit(solution)/shard_map/ppermute | solution.py:336
  345.0 11.7 %copy-start.6 = (bf16[4,408,656]{2,1,0:T(8,128)(2,1)S(1)}, bf16[4,408,656]{2,1,0:T(8,128)(2,1)}, u32[]{:S(2)}) copy-start(bf16[4,408,656]{2,1,0:T(8,128)(2,1)} %copy-done.5) | copy-start | bytes 6423556
  349.4 7.4 %copy-start.24 = (f32[408,1024]{1,0:T(8,128)S(1)}, f32[408,1024]{1,0:T(8,128)}, u32[]{:S(2)}) copy-start(f32[408,1024]{1,0:T(8,128)} %copy-done.22) | copy-start | bytes 5013508
  349.4 31.3 %collective-permute-start.14 = (bf16[2,2,2,2,128,512]{4,5,0,1,3,2:T(8,128)(2,1)}, bf16[2,2,2,2,128,512]{4,5,0,1,3,2:T(8,128)(2,1)}, u32[]{:S(2)}, u32[]{:S(2)}) collective-permute-start(bf16[2,2,2,2,128,512]{4,5,0,1,3,2:T(8,128)(2,1)} %bitcast.118), channel_id=1, source_target_pairs={{0,4},{4,0},{8,12},{12,8},{16,20},{20,16},{24,28},{28,24},{1,5},{5... | collective-permute-start | bytes 6291464 | tf_op jit(solution)/shard_map/ppermute | solution.py:238
  356.6 13.5 %collective-permute-start.4 = (f32[2,1024]{1,0:T(2,128)S(1)}, f32[2,1024]{1,0:T(2,128)S(1)}, u32[]{:S(2)}, u32[]{:S(2)}) collective-permute-start(f32[2,1024]{1,0:T(2,128)S(1)} %pad_maximum_fusion.3), channel_id=1, source_target_pairs={{0,4},{4,0},{8,12},{12,8},{16,20},{20,16},{24,28},{28,24},{1,5},{5... | collective-permute-start | bytes 24584 | tf_op jit(solution)/shard_map/ppermute | solution.py:216
  363.3 4.3 copy-start.28
  367.6 4.8 copy-start.35
  370.0 4.1 collective-permute-start.5
  374.1 6.6 %copy-start.27 = (bf16[2,2,2,2,1,128,512]{5,6,0,1,3,2,4:T(8,128)(2,1)S(1)}, bf16[2,2,2,2,1,128,512]{5,6,0,1,3,2,4:T(8,128)(2,1)}, u32[]{:S(2)}) copy-start(bf16[2,2,2,2,1,128,512]{5,6,0,1,3,2,4:T(8,128)(2,1)} %copy.92) | copy-start | bytes 6291460
  374.1 11.5 %collective-permute-start.6 = (f32[2,1024]{1,0:T(2,128)S(1)}, f32[2,1024]{1,0:T(2,128)S(1)}, u32[]{:S(2)}, u32[]{:S(2)}) collective-permute-start(f32[2,1024]{1,0:T(2,128)S(1)} %fusion.100), channel_id=1, source_target_pairs={{0,16},{4,20},{8,24},{12,28},{16,0},{20,4},{24,8},{28,12},{1,17},{... | collective-permute-start | bytes 24584 | tf_op jit(solution)/shard_map/ppermute | solution.py:216
  380.5 47.9 %collective-permute-start.10 = (bf16[2,2,2,128,512]{3,4,0,1,2:T(8,128)(2,1)S(1)}, bf16[2,2,2,128,512]{3,4,0,1,2:T(8,128)(2,1)S(1)}, u32[]{:S(2)}, u32[]{:S(2)}) collective-permute-start(bf16[2,2,2,128,512]{3,4,0,1,2:T(8,128)(2,1)S(1)} %dynamic-slice_bitcast_fusion.1), channel_id=1, source_target_pairs={{0,8},{4,12},{8,0},{12,4},{16,24},{20,28},{24,16},{28,20},{1,9},{5... | collective-permute-start | bytes 3145736 | tf_op jit(solution)/shard_map/ppermute | solution.py:238
  383.1 6.4 %copy-start.26 = (f32[408,1024]{1,0:T(8,128)S(1)}, f32[408,1024]{1,0:T(8,128)}, u32[]{:S(2)}) copy-start(f32[408,1024]{1,0:T(8,128)} %copy-done.25) | copy-start | bytes 5013508
  383.1 46.6 %collective-permute-start.15 = (bf16[2,2,2,128,512]{3,4,0,1,2:T(8,128)(2,1)S(1)}, bf16[2,2,2,128,512]{3,4,0,1,2:T(8,128)(2,1)S(1)}, u32[]{:S(2)}, u32[]{:S(2)}) collective-permute-start(bf16[2,2,2,128,512]{3,4,0,1,2:T(8,128)(2,1)S(1)} %dynamic-slice_bitcast_fusion), channel_id=1, source_target_pairs={{0,16},{4,20},{8,24},{12,28},{16,0},{20,4},{24,8},{28,12},{1,17},{... | collective-permute-start | bytes 3145736 | tf_op jit(solution)/shard_map/ppermute | solution.py:238
  385.7 3.7 collective-permute-start.7
  389.4 4.7 collective-permute-start.8
  428.7 19.2 %collective-permute-start.11 = (bf16[2,2,128,512]{2,3,0,1:T(8,128)(2,1)S(1)}, bf16[2,2,128,512]{2,3,0,1:T(8,128)(2,1)S(1)}, u32[]{:S(2)}, u32[]{:S(2)}) collective-permute-start(bf16[2,2,128,512]{2,3,0,1:T(8,128)(2,1)S(1)} %dynamic-slice_bitcast_fusion.3), channel_id=1, source_target_pairs={{0,16},{4,20},{8,24},{12,28},{16,0},{20,4},{24,8},{28,12},{1,17},{... | collective-permute-start | bytes 1572872 | tf_op jit(solution)/shard_map/ppermute | solution.py:238
  430.0 25.7 %collective-permute-start.16 = (bf16[2,2,128,512]{2,3,0,1:T(8,128)(2,1)S(1)}, bf16[2,2,128,512]{2,3,0,1:T(8,128)(2,1)S(1)}, u32[]{:S(2)}, u32[]{:S(2)}) collective-permute-start(bf16[2,2,128,512]{2,3,0,1:T(8,128)(2,1)S(1)} %dynamic-slice_bitcast_fusion.2), channel_id=1, source_target_pairs={{0,8},{4,12},{8,0},{12,4},{16,24},{20,28},{24,16},{28,20},{1,9},{5... | collective-permute-start | bytes 1572872 | tf_op jit(solution)/shard_map/ppermute | solution.py:238
  448.1 8.4 %collective-permute-start.12 = (bf16[2,128,512]{1,2,0:T(8,128)(2,1)S(1)}, bf16[2,128,512]{1,2,0:T(8,128)(2,1)S(1)}, u32[]{:S(2)}, u32[]{:S(2)}) collective-permute-start(bf16[2,128,512]{1,2,0:T(8,128)(2,1)S(1)} %dynamic-slice_bitcast_fusion.5), channel_id=1, source_target_pairs={{0,1},{1,0},{2,3},{3,2},{4,5},{5,4},{6,7},{7,6},{8,9},{9,8},{10,11... | collective-permute-start | bytes 786440 | tf_op jit(solution)/shard_map/ppermute | solution.py:238
  455.8 12.8 %collective-permute-start.17 = (bf16[2,128,512]{1,2,0:T(8,128)(2,1)S(1)}, bf16[2,128,512]{1,2,0:T(8,128)(2,1)S(1)}, u32[]{:S(2)}, u32[]{:S(2)}) collective-permute-start(bf16[2,128,512]{1,2,0:T(8,128)(2,1)S(1)} %dynamic-slice_bitcast_fusion.4), channel_id=1, source_target_pairs={{0,1},{1,0},{2,3},{3,2},{4,5},{5,4},{6,7},{7,6},{8,9},{9,8},{10,11... | collective-permute-start | bytes 786440 | tf_op jit(solution)/shard_map/ppermute | solution.py:238
  456.6 12.2 %collective-permute-start.13 = (bf16[128,512]{0,1:T(8,128)(2,1)S(1)}, bf16[128,512]{0,1:T(8,128)(2,1)S(1)}, u32[]{:S(2)}, u32[]{:S(2)}) collective-permute-start(bf16[128,512]{0,1:T(8,128)(2,1)S(1)} %dynamic-slice_bitcast_fusion.7), channel_id=1, source_target_pairs={{0,2},{1,3},{2,0},{3,1},{4,6},{5,7},{6,4},{7,5},{8,10},{9,11},{10,... | collective-permute-start | bytes 393224 | tf_op jit(solution)/shard_map/ppermute | solution.py:238
  468.8 8.4 %collective-permute-start.18 = (bf16[128,512]{0,1:T(8,128)(2,1)S(1)}, bf16[128,512]{0,1:T(8,128)(2,1)S(1)}, u32[]{:S(2)}, u32[]{:S(2)}) collective-permute-start(bf16[128,512]{0,1:T(8,128)(2,1)S(1)} %dynamic-slice_bitcast_fusion.6), channel_id=1, source_target_pairs={{0,2},{1,3},{2,0},{3,1},{4,6},{5,7},{6,4},{7,5},{8,10},{9,11},{10,... | collective-permute-start | bytes 393224 | tf_op jit(solution)/shard_map/ppermute | solution.py:238
  478.2 9.8 %copy-start.1 = (bf16[1024,2,656]{0,2,1:T(8,128)(2,1)S(1)}, bf16[1024,2,656]{0,2,1:T(8,128)(2,1)}, u32[]{:S(2)}) copy-start(bf16[1024,2,656]{0,2,1:T(8,128)(2,1)} %param.15) | copy-start | bytes 8060932
  480.9 4.0 copy-start.32
  (13 other events, 34.8 us)
Sparse Core Ops, SparseCore 0:
  15.4 163.6 all-gather.1
  259.9 220.9 reduce-scatter.1
